TPU v7x, 128 devices: a whole 4x4x4 slice. The times are simulated.
128 devices in a mesh: item: 8 (over x_lo, z), user: 16 (over x_hi, y, core).
Axes of the slice: x: 4 (x_hi: 2, x_lo: 2; x = x_hi * 2 + x_lo), y: 4, z: 4, core: 2. Of those that a mesh axis runs over, the one named last changes fastest.
Arguments:
- history: bfloat16 [128, 1024, 512], P(('item', 'user')), may hold values from -6 to 6
- hist_len: int32 [128], P(('item', 'user')), may hold values from 256 to 1024, as said below
- cand_ids: int32 [128, 128], P(('item', 'user')), may hold values from 0 to 383, as said below
- cand_lists: int32 [128, 4], P(('item', 'user')), may hold values from 0 to 15, as said below
- item_table: bfloat16 [6144, 512], P('user', 'item'), may hold values from -6 to 6
- w_in: bfloat16 [512, 2048], replicated, may hold values from -0.25 to 0.25
- w_out: bfloat16 [512, 512], replicated, may hold values from -0.25 to 0.25
- grad_cand: bfloat16 [128, 128, 512], P(('item', 'user')), may hold values from -6 to 6
Outputs:
- hist_out: bfloat16 [128, 1024, 512], P(('item', 'user'))
- cand_out: bfloat16 [128, 128, 512], P(('item', 'user'))
- table_grad: float32 [6144, 512], P('user', 'item')
Inputs may be any that keep to these rules, and one draw needn't show every extreme that they name: `hist_len`: some user has exactly 1024 events; positions at or past a user's length are padding. `cand_ids`: the 128 ids of one user are different. `cand_lists`: the 4 entries of user g are different and none equals g mod 16.
All inputs are finite; a program needn't handle non-finite values.
Results may differ from a plain program's by a relative error of at most 0.013.
Values may be sent and summed in bfloat16 or wider, within the bound.
A program may use at most 64 MiB of HBM per device.

v0:
```python
import jax
import jax.numpy as jnp
from jax import lax
from jax.sharding import PartitionSpec as P

H = 8


NORM_EPS = 1e-05


def from_behind(block, axis, distance):
    devices = range(lax.axis_size(axis))
    route = [((i - distance) % len(devices), i) for i in devices]
    return lax.ppermute(block, axis, route)


def silu_slope(pre_act):
    sigmoid = jax.nn.sigmoid(pre_act)
    return sigmoid * (1.0 + pre_act * (1.0 - sigmoid))


def normalize(rows_in):
    centred = rows_in - jnp.mean(rows_in, axis=-1, keepdims=True)
    inv_dev = lax.rsqrt(jnp.mean(centred * centred, axis=-1, keepdims=True) + NORM_EPS)
    return (centred * inv_dev, inv_dev)


def history_layer(events, length, projected, w_out):
    event_rows = events.shape[0]
    model_width = events.shape[1]
    head_size = model_width // H
    att_scale = head_size ** (-0.5)
    block_rows = min(512, event_rows)
    u_part = projected[:, :model_width]
    heads_v = projected[:, model_width : 2 * model_width].reshape(event_rows, H, head_size)
    heads_q = projected[:, 2 * model_width : 3 * model_width].reshape(event_rows, H, head_size)
    heads_k = projected[:, 3 * model_width :].reshape(event_rows, H, head_size)
    block_total = (length + block_rows - 1) // block_rows

    def query_block(q_index, result):
        q_start = q_index * block_rows
        q_tile = lax.dynamic_slice_in_dim(heads_q, q_start, block_rows, 0)
        q_pos = q_start + jnp.arange(block_rows)

        def key_block(k_index, running):
            k_start = k_index * block_rows
            k_tile = lax.dynamic_slice_in_dim(heads_k, k_start, block_rows, 0)
            v_tile = lax.dynamic_slice_in_dim(heads_v, k_start, block_rows, 0)
            k_pos = k_start + jnp.arange(block_rows)
            scores = (
                jnp.einsum("qhd,khd->hqk", q_tile, k_tile, preferred_element_type=jnp.float32)
                * att_scale
            )
            allowed = (k_pos[None, :] <= q_pos[:, None]) & (k_pos[None, :] < length)
            weights = jnp.where(allowed[None], jax.nn.silu(scores), 0.0).astype(jnp.bfloat16)
            return running + jnp.einsum(
                "hqk,khd->qhd", weights, v_tile, preferred_element_type=jnp.float32
            )

        attended = lax.fori_loop(
            0, q_index + 1, key_block, jnp.zeros((block_rows, H, head_size), jnp.float32)
        )
        normed = normalize(attended.reshape(block_rows, model_width))[0]
        u_tile = lax.dynamic_slice_in_dim(u_part, q_start, block_rows, 0)
        mixed_rows = (normed * u_tile.astype(jnp.float32)).astype(jnp.bfloat16)
        x_tile = lax.dynamic_slice_in_dim(events, q_start, block_rows, 0)
        layer_out = jnp.dot(mixed_rows, w_out, preferred_element_type=jnp.float32) + x_tile.astype(
            jnp.float32
        )
        layer_out = jnp.where((q_pos < length)[:, None], layer_out, 0.0).astype(jnp.bfloat16)
        return lax.dynamic_update_slice_in_dim(result, layer_out, q_start, 0)

    return lax.fori_loop(0, block_total, query_block, jnp.zeros_like(events))


def candidate_pass(
    cand_q, cand_u, cand_emb, keys_k, keys_v, valid_keys, skip_rows, w_out, grad_rows
):
    cand_rows = cand_q.shape[0]
    model_width = cand_q.shape[1]
    head_size = model_width // H
    att_scale = head_size ** (-0.5)
    heads_q = cand_q.reshape(cand_rows, H, head_size)
    heads_k = keys_k.reshape(-1, H, head_size)
    heads_v = keys_v.reshape(-1, H, head_size)
    scores = (
        jnp.einsum("qhd,khd->hqk", heads_q, heads_k, preferred_element_type=jnp.float32) * att_scale
    )
    weights = jnp.where(valid_keys[None, None, :], jax.nn.silu(scores), 0.0).astype(jnp.bfloat16)
    attended = jnp.einsum(
        "hqk,khd->qhd", weights, heads_v, preferred_element_type=jnp.float32
    ).reshape(cand_rows, model_width)
    normed, inv_dev = normalize(attended)
    u_rows = cand_u.astype(jnp.float32)
    mixed_rows = (normed * u_rows).astype(jnp.bfloat16)
    layer_out = (
        jnp.dot(mixed_rows, w_out, preferred_element_type=jnp.float32)
        + cand_emb.astype(jnp.float32)
    ).astype(jnp.bfloat16)
    grad_mixed = jnp.einsum("rd,ed->re", grad_rows, w_out, preferred_element_type=jnp.float32)
    grad_u = grad_mixed * normed
    grad_normed = grad_mixed * u_rows
    grad_att = inv_dev * (
        grad_normed
        - jnp.mean(grad_normed, axis=-1, keepdims=True)
        - normed * jnp.mean(grad_normed * normed, axis=-1, keepdims=True)
    )
    grad_att = grad_att.astype(jnp.bfloat16).reshape(cand_rows, H, head_size)
    grad_weights = jnp.einsum("qhd,khd->hqk", grad_att, heads_v, preferred_element_type=jnp.float32)
    grad_scores = (
        jnp.where(valid_keys[None, None, :], grad_weights * silu_slope(scores), 0.0) * att_scale
    ).astype(jnp.bfloat16)
    grad_q = jnp.einsum(
        "hqk,khd->qhd", grad_scores, heads_k, preferred_element_type=jnp.float32
    ).reshape(cand_rows, model_width)
    grad_k = jnp.einsum(
        "hqk,qhd->khd", grad_scores[:, :, skip_rows:], heads_q, preferred_element_type=jnp.float32
    ).reshape(-1, model_width)
    grad_v = jnp.einsum(
        "hqk,qhd->khd", weights[:, :, skip_rows:], grad_att, preferred_element_type=jnp.float32
    ).reshape(-1, model_width)
    return (layer_out, grad_u, grad_q, grad_k, grad_v)


def local(history, hist_len, cand_ids, cand_lists, item_table, w_in, w_out, grad_cand):
    events = history[0]
    length = hist_len[0]
    own_ids = cand_ids[0]
    my_lists = cand_lists[0]
    grad_rows = grad_cand[0]
    event_rows = events.shape[0]
    model_width = events.shape[1]
    cand_count = own_ids.shape[0]
    slot_count = my_lists.shape[0]
    part_rows = item_table.shape[0]
    cycle_size = lax.axis_size("user")
    cycle_pos = lax.axis_index("user")
    catalogue = jnp.arange(part_rows, dtype=jnp.int32)
    own_hot = (own_ids[:, None] == catalogue[None, :]).astype(jnp.bfloat16)
    cand_emb = jnp.dot(
        own_hot,
        lax.all_gather(item_table, "item", axis=1, tiled=True),
        preferred_element_type=jnp.float32,
    ).astype(jnp.bfloat16)
    projected = jax.nn.silu(jnp.dot(events, w_in, preferred_element_type=jnp.float32)).astype(
        jnp.bfloat16
    )
    cand_pre = jnp.dot(cand_emb, w_in, preferred_element_type=jnp.float32)
    cand_proj = jax.nn.silu(cand_pre).astype(jnp.bfloat16)
    cand_u = cand_proj[:, :model_width]
    cand_v = cand_proj[:, model_width : 2 * model_width]
    cand_q = cand_proj[:, 2 * model_width : 3 * model_width]
    cand_k = cand_proj[:, 3 * model_width :]
    block_kv = jnp.concatenate([cand_k, cand_v], 1)
    held_slots = jnp.zeros((slot_count, cand_count, 2 * model_width), jnp.bfloat16)

    def store_block(slots_now, moving, source):
        return jnp.where((my_lists == source)[:, None, None], moving[None], slots_now)

    def forward_turn(turn_no, carried):
        moving, slots_now = carried
        moving = from_behind(moving, "user", 1)
        return (moving, store_block(slots_now, moving, (cycle_pos - turn_no) % cycle_size))

    held_slots = lax.fori_loop(1, cycle_size, forward_turn, (block_kv, held_slots))[1]
    hist_out = history_layer(events, length, projected, w_out)
    slot_k = held_slots[:, :, :model_width].reshape(slot_count * cand_count, model_width)
    slot_v = held_slots[:, :, model_width:].reshape(slot_count * cand_count, model_width)
    keys_k = jnp.concatenate([projected[:, 3 * model_width :], cand_k, slot_k], 0)
    keys_v = jnp.concatenate([projected[:, model_width : 2 * model_width], cand_v, slot_v], 0)
    valid_keys = jnp.concatenate(
        [jnp.arange(event_rows) < length, jnp.ones(((1 + slot_count) * cand_count,), dtype=bool)], 0
    )
    cand_out, grad_u, grad_q, grad_k, grad_v = candidate_pass(
        cand_q, cand_u, cand_emb, keys_k, keys_v, valid_keys, event_rows, w_out, grad_rows
    )
    grad_own = jnp.concatenate([grad_k[:cand_count], grad_v[:cand_count]], 1)
    grad_slots = jnp.concatenate(
        [
            grad_k[cand_count:].reshape(slot_count, cand_count, model_width),
            grad_v[cand_count:].reshape(slot_count, cand_count, model_width),
        ],
        2,
    )

    def slot_terms(owner):
        matched = my_lists == owner % cycle_size
        return jnp.sum(jnp.where(matched[:, None, None], grad_slots, 0.0), 0)

    def give_back(turn_no, running):
        running = from_behind(running.astype(jnp.bfloat16), "user", 1).astype(running.dtype)
        return running + slot_terms(cycle_pos - turn_no)

    grad_home = lax.fori_loop(1, cycle_size + 1, give_back, grad_own)
    grad_proj = jnp.concatenate(
        [grad_u, grad_home[:, model_width:], grad_q, grad_home[:, :model_width]], 1
    )
    grad_pre = (grad_proj * silu_slope(cand_pre)).astype(jnp.bfloat16)
    grad_emb = jnp.einsum(
        "rf,df->rd", grad_pre, w_in, preferred_element_type=jnp.float32
    ) + grad_rows.astype(jnp.float32)
    table_terms = jnp.einsum(
        "cv,cd->vd", own_hot.astype(jnp.float32), grad_emb, precision=lax.Precision.HIGHEST
    )
    table_grad = lax.psum_scatter(
        table_terms.astype(jnp.bfloat16), "item", scatter_dimension=1, tiled=True
    ).astype(jnp.float32)
    return (hist_out[None], cand_out[None], table_grad)


def solution(mesh):
    in_specs = (
        P(("item", "user"), None, None),
        P(("item", "user")),
        P(("item", "user"), None),
        P(("item", "user"), None),
        P("user", "item"),
        P(),
        P(),
        P(("item", "user"), None, None),
    )
    out_specs = (
        P(("item", "user"), None, None),
        P(("item", "user"), None, None),
        P("user", "item"),
    )
    return jax.shard_map(local, mesh=mesh, in_specs=in_specs, out_specs=out_specs, check_vma=False)
```

profile of v0, /device:TPU:32, one launch (start us, length us, event | category | flops | bytes accessed | tf_op | source)
XLA Modules:
  0.0 472.2 jit_solution(8002575875772738989)
XLA Ops:
  7.2 30.1 %all_gather.3 = bf16[384,512]{0,1:T(8,128)(2,1)S(1)} all-gather(bf16[384,64]{0,1:T(8,128)(2,1)} %param.20), channel_id=1, replica_groups=mesh['item'=8,'user'=16] {'item'}, dimensions={1}, use_global_device_ids=true | all-gather | bytes 442368 | tf_op jit(solution)/shard_map/all_gather | solution.py:143
  55.3 161.5 %while.57 = (s32[]{:T(128)}, bf16[128,1024]{1,0:T(8,128)(2,1)}, bf16[4,128,1024]{2,1,0:T(8,128)(2,1)S(1)}, s32[]{:T(128)}, s32[4]{0:T(128)S(1)}, /*index=5*/s32[]{:T(128)}, s32[]{:T(128)}, s32[]{:T(128)}, s32[]{:T(128)}) while((s32[]{:T(128)}, bf16[128,1024]{1,0:T(8,128)(2,1)}, bf16[4,128,1024]{2,1,0:T(8,128)(2,1)S(1)}, s32[]{:T(128)}, ...), condition=%wide.region_7.8_spmd.clone, body=%wide.region_6.7_spmd.clone.sunk | while | flops 1048595 | bytes 3932460 | solution.py:166
  55.3 9.6 %collective-permute-done.1 = bf16[128,1024]{1,0:T(8,128)(2,1)S(1)} collective-permute-done((bf16[128,1024]{1,0:T(8,128)(2,1)}, bf16[128,1024]{1,0:T(8,128)(2,1)S(1)}, u32[]{:S(2)}, u32[]{:S(2)}) %collective-permute-start.1) | collective-permute-done | bytes 262176 | tf_op jit(solution)/shard_map/while/body/eval_jaxpr/ppermute | solution.py:15
  66.1 9.6 %collective-permute-done.1 = bf16[128,1024]{1,0:T(8,128)(2,1)S(1)} collective-permute-done((bf16[128,1024]{1,0:T(8,128)(2,1)}, bf16[128,1024]{1,0:T(8,128)(2,1)S(1)}, u32[]{:S(2)}, u32[]{:S(2)}) %collective-permute-start.1) | collective-permute-done | bytes 262176 | tf_op jit(solution)/shard_map/while/body/eval_jaxpr/ppermute | solution.py:15
  76.9 9.6 %collective-permute-done.1 = bf16[128,1024]{1,0:T(8,128)(2,1)S(1)} collective-permute-done((bf16[128,1024]{1,0:T(8,128)(2,1)}, bf16[128,1024]{1,0:T(8,128)(2,1)S(1)}, u32[]{:S(2)}, u32[]{:S(2)}) %collective-permute-start.1) | collective-permute-done | bytes 262176 | tf_op jit(solution)/shard_map/while/body/eval_jaxpr/ppermute | solution.py:15
  87.7 9.6 %collective-permute-done.1 = bf16[128,1024]{1,0:T(8,128)(2,1)S(1)} collective-permute-done((bf16[128,1024]{1,0:T(8,128)(2,1)}, bf16[128,1024]{1,0:T(8,128)(2,1)S(1)}, u32[]{:S(2)}, u32[]{:S(2)}) %collective-permute-start.1) | collective-permute-done | bytes 262176 | tf_op jit(solution)/shard_map/while/body/eval_jaxpr/ppermute | solution.py:15
  98.4 9.6 %collective-permute-done.1 = bf16[128,1024]{1,0:T(8,128)(2,1)S(1)} collective-permute-done((bf16[128,1024]{1,0:T(8,128)(2,1)}, bf16[128,1024]{1,0:T(8,128)(2,1)S(1)}, u32[]{:S(2)}, u32[]{:S(2)}) %collective-permute-start.1) | collective-permute-done | bytes 262176 | tf_op jit(solution)/shard_map/while/body/eval_jaxpr/ppermute | solution.py:15
  109.2 9.6 %collective-permute-done.1 = bf16[128,1024]{1,0:T(8,128)(2,1)S(1)} collective-permute-done((bf16[128,1024]{1,0:T(8,128)(2,1)}, bf16[128,1024]{1,0:T(8,128)(2,1)S(1)}, u32[]{:S(2)}, u32[]{:S(2)}) %collective-permute-start.1) | collective-permute-done | bytes 262176 | tf_op jit(solution)/shard_map/while/body/eval_jaxpr/ppermute | solution.py:15
  120.0 9.6 %collective-permute-done.1 = bf16[128,1024]{1,0:T(8,128)(2,1)S(1)} collective-permute-done((bf16[128,1024]{1,0:T(8,128)(2,1)}, bf16[128,1024]{1,0:T(8,128)(2,1)S(1)}, u32[]{:S(2)}, u32[]{:S(2)}) %collective-permute-start.1) | collective-permute-done | bytes 262176 | tf_op jit(solution)/shard_map/while/body/eval_jaxpr/ppermute | solution.py:15
  130.8 9.6 %collective-permute-done.1 = bf16[128,1024]{1,0:T(8,128)(2,1)S(1)} collective-permute-done((bf16[128,1024]{1,0:T(8,128)(2,1)}, bf16[128,1024]{1,0:T(8,128)(2,1)S(1)}, u32[]{:S(2)}, u32[]{:S(2)}) %collective-permute-start.1) | collective-permute-done | bytes 262176 | tf_op jit(solution)/shard_map/while/body/eval_jaxpr/ppermute | solution.py:15
  141.5 9.6 %collective-permute-done.1 = bf16[128,1024]{1,0:T(8,128)(2,1)S(1)} collective-permute-done((bf16[128,1024]{1,0:T(8,128)(2,1)}, bf16[128,1024]{1,0:T(8,128)(2,1)S(1)}, u32[]{:S(2)}, u32[]{:S(2)}) %collective-permute-start.1) | collective-permute-done | bytes 262176 | tf_op jit(solution)/shard_map/while/body/eval_jaxpr/ppermute | solution.py:15
  152.3 9.6 %collective-permute-done.1 = bf16[128,1024]{1,0:T(8,128)(2,1)S(1)} collective-permute-done((bf16[128,1024]{1,0:T(8,128)(2,1)}, bf16[128,1024]{1,0:T(8,128)(2,1)S(1)}, u32[]{:S(2)}, u32[]{:S(2)}) %collective-permute-start.1) | collective-permute-done | bytes 262176 | tf_op jit(solution)/shard_map/while/body/eval_jaxpr/ppermute | solution.py:15
  163.1 9.6 %collective-permute-done.1 = bf16[128,1024]{1,0:T(8,128)(2,1)S(1)} collective-permute-done((bf16[128,1024]{1,0:T(8,128)(2,1)}, bf16[128,1024]{1,0:T(8,128)(2,1)S(1)}, u32[]{:S(2)}, u32[]{:S(2)}) %collective-permute-start.1) | collective-permute-done | bytes 262176 | tf_op jit(solution)/shard_map/while/body/eval_jaxpr/ppermute | solution.py:15
  173.8 9.6 %collective-permute-done.1 = bf16[128,1024]{1,0:T(8,128)(2,1)S(1)} collective-permute-done((bf16[128,1024]{1,0:T(8,128)(2,1)}, bf16[128,1024]{1,0:T(8,128)(2,1)S(1)}, u32[]{:S(2)}, u32[]{:S(2)}) %collective-permute-start.1) | collective-permute-done | bytes 262176 | tf_op jit(solution)/shard_map/while/body/eval_jaxpr/ppermute | solution.py:15
  184.6 9.6 %collective-permute-done.1 = bf16[128,1024]{1,0:T(8,128)(2,1)S(1)} collective-permute-done((bf16[128,1024]{1,0:T(8,128)(2,1)}, bf16[128,1024]{1,0:T(8,128)(2,1)S(1)}, u32[]{:S(2)}, u32[]{:S(2)}) %collective-permute-start.1) | collective-permute-done | bytes 262176 | tf_op jit(solution)/shard_map/while/body/eval_jaxpr/ppermute | solution.py:15
  195.4 9.6 %collective-permute-done.1 = bf16[128,1024]{1,0:T(8,128)(2,1)S(1)} collective-permute-done((bf16[128,1024]{1,0:T(8,128)(2,1)}, bf16[128,1024]{1,0:T(8,128)(2,1)S(1)}, u32[]{:S(2)}, u32[]{:S(2)}) %collective-permute-start.1) | collective-permute-done | bytes 262176 | tf_op jit(solution)/shard_map/while/body/eval_jaxpr/ppermute | solution.py:15
  206.2 9.6 %collective-permute-done.1 = bf16[128,1024]{1,0:T(8,128)(2,1)S(1)} collective-permute-done((bf16[128,1024]{1,0:T(8,128)(2,1)}, bf16[128,1024]{1,0:T(8,128)(2,1)S(1)}, u32[]{:S(2)}, u32[]{:S(2)}) %collective-permute-start.1) | collective-permute-done | bytes 262176 | tf_op jit(solution)/shard_map/while/body/eval_jaxpr/ppermute | solution.py:15
  261.7 153.9 %while.56 = (s32[]{:T(128)}, f32[128,1024]{1,0:T(8,128)S(1)}, s32[]{:T(128)}, s32[4]{0:T(128)S(1)}, f32[4,128,1024]{2,1,0:T(8,128)}, /*index=5*/s32[]{:T(128)}, s32[]{:T(128)}, s32[]{:T(128)}, s32[]{:T(128)}) while((s32[]{:T(128)}, f32[128,1024]{1,0:T(8,128)S(1)}, s32[]{:T(128)}, s32[4]{0:T(128)S(1)}, f32[4,128,1024]{2,1,0:T(8,128)}, ...), condition=%wide.region_14.15_spmd, body=%wide.region_12.14_spmd.sunk | while | flops 1310738 | bytes 5767450 | solution.py:195
  263.8 7.4 %collective-permute-done = bf16[128,1024]{1,0:T(8,128)(2,1)S(1)} collective-permute-done((bf16[128,1024]{1,0:T(8,128)(2,1)S(1)}, bf16[128,1024]{1,0:T(8,128)(2,1)S(1)}, u32[]{:S(2)}, u32[]{:S(2)}) %collective-permute-start) | collective-permute-done | bytes 262176 | tf_op jit(solution)/shard_map/while/body/eval_jaxpr/ppermute | solution.py:15
  273.4 7.4 %collective-permute-done = bf16[128,1024]{1,0:T(8,128)(2,1)S(1)} collective-permute-done((bf16[128,1024]{1,0:T(8,128)(2,1)S(1)}, bf16[128,1024]{1,0:T(8,128)(2,1)S(1)}, u32[]{:S(2)}, u32[]{:S(2)}) %collective-permute-start) | collective-permute-done | bytes 262176 | tf_op jit(solution)/shard_map/while/body/eval_jaxpr/ppermute | solution.py:15
  283.0 7.4 %collective-permute-done = bf16[128,1024]{1,0:T(8,128)(2,1)S(1)} collective-permute-done((bf16[128,1024]{1,0:T(8,128)(2,1)S(1)}, bf16[128,1024]{1,0:T(8,128)(2,1)S(1)}, u32[]{:S(2)}, u32[]{:S(2)}) %collective-permute-start) | collective-permute-done | bytes 262176 | tf_op jit(solution)/shard_map/while/body/eval_jaxpr/ppermute | solution.py:15
  292.6 7.4 %collective-permute-done = bf16[128,1024]{1,0:T(8,128)(2,1)S(1)} collective-permute-done((bf16[128,1024]{1,0:T(8,128)(2,1)S(1)}, bf16[128,1024]{1,0:T(8,128)(2,1)S(1)}, u32[]{:S(2)}, u32[]{:S(2)}) %collective-permute-start) | collective-permute-done | bytes 262176 | tf_op jit(solution)/shard_map/while/body/eval_jaxpr/ppermute | solution.py:15
  302.2 7.4 %collective-permute-done = bf16[128,1024]{1,0:T(8,128)(2,1)S(1)} collective-permute-done((bf16[128,1024]{1,0:T(8,128)(2,1)S(1)}, bf16[128,1024]{1,0:T(8,128)(2,1)S(1)}, u32[]{:S(2)}, u32[]{:S(2)}) %collective-permute-start) | collective-permute-done | bytes 262176 | tf_op jit(solution)/shard_map/while/body/eval_jaxpr/ppermute | solution.py:15
  311.8 7.4 %collective-permute-done = bf16[128,1024]{1,0:T(8,128)(2,1)S(1)} collective-permute-done((bf16[128,1024]{1,0:T(8,128)(2,1)S(1)}, bf16[128,1024]{1,0:T(8,128)(2,1)S(1)}, u32[]{:S(2)}, u32[]{:S(2)}) %collective-permute-start) | collective-permute-done | bytes 262176 | tf_op jit(solution)/shard_map/while/body/eval_jaxpr/ppermute | solution.py:15
  321.4 7.4 %collective-permute-done = bf16[128,1024]{1,0:T(8,128)(2,1)S(1)} collective-permute-done((bf16[128,1024]{1,0:T(8,128)(2,1)S(1)}, bf16[128,1024]{1,0:T(8,128)(2,1)S(1)}, u32[]{:S(2)}, u32[]{:S(2)}) %collective-permute-start) | collective-permute-done | bytes 262176 | tf_op jit(solution)/shard_map/while/body/eval_jaxpr/ppermute | solution.py:15
  340.7 7.4 %collective-permute-done = bf16[128,1024]{1,0:T(8,128)(2,1)S(1)} collective-permute-done((bf16[128,1024]{1,0:T(8,128)(2,1)S(1)}, bf16[128,1024]{1,0:T(8,128)(2,1)S(1)}, u32[]{:S(2)}, u32[]{:S(2)}) %collective-permute-start) | collective-permute-done | bytes 262176 | tf_op jit(solution)/shard_map/while/body/eval_jaxpr/ppermute | solution.py:15
  350.3 7.4 %collective-permute-done = bf16[128,1024]{1,0:T(8,128)(2,1)S(1)} collective-permute-done((bf16[128,1024]{1,0:T(8,128)(2,1)S(1)}, bf16[128,1024]{1,0:T(8,128)(2,1)S(1)}, u32[]{:S(2)}, u32[]{:S(2)}) %collective-permute-start) | collective-permute-done | bytes 262176 | tf_op jit(solution)/shard_map/while/body/eval_jaxpr/ppermute | solution.py:15
  359.9 7.4 %collective-permute-done = bf16[128,1024]{1,0:T(8,128)(2,1)S(1)} collective-permute-done((bf16[128,1024]{1,0:T(8,128)(2,1)S(1)}, bf16[128,1024]{1,0:T(8,128)(2,1)S(1)}, u32[]{:S(2)}, u32[]{:S(2)}) %collective-permute-start) | collective-permute-done | bytes 262176 | tf_op jit(solution)/shard_map/while/body/eval_jaxpr/ppermute | solution.py:15
  379.1 7.4 %collective-permute-done = bf16[128,1024]{1,0:T(8,128)(2,1)S(1)} collective-permute-done((bf16[128,1024]{1,0:T(8,128)(2,1)S(1)}, bf16[128,1024]{1,0:T(8,128)(2,1)S(1)}, u32[]{:S(2)}, u32[]{:S(2)}) %collective-permute-start) | collective-permute-done | bytes 262176 | tf_op jit(solution)/shard_map/while/body/eval_jaxpr/ppermute | solution.py:15
  388.7 7.4 %collective-permute-done = bf16[128,1024]{1,0:T(8,128)(2,1)S(1)} collective-permute-done((bf16[128,1024]{1,0:T(8,128)(2,1)S(1)}, bf16[128,1024]{1,0:T(8,128)(2,1)S(1)}, u32[]{:S(2)}, u32[]{:S(2)}) %collective-permute-start) | collective-permute-done | bytes 262176 | tf_op jit(solution)/shard_map/while/body/eval_jaxpr/ppermute | solution.py:15
  423.5 38.3 %while.55 = (s32[]{:T(128)}, bf16[1024,512]{1,0:T(8,128)(2,1)}, s32[]{:T(128)}, s32[]{:T(128)}, bf16[1024,8,64]{0,2,1:T(8,128)(2,1)}, /*index=5*/bf16[1024,8,64]...) while((s32[]{:T(128)}, bf16[1024,512]{1,0:T(8,128)(2,1)}, ...), condition=%wide.region_5.6_spmd, body=%wide.region_0.5_spmd.sunk | while | flops 824184320 | bytes 14710306 | solution.py:74
  441.9 11.3 %while.58 = (s32[]{:T(128)}, f32[512,8,64]{0,2,1:T(8,128)S(1)}, s32[]{:T(128)}, bf16[1024,8,64]{0,2,1:T(8,128)(2,1)}, s32[]{:T(128)}, /*index=5*/bf16[1024,8,64]...) while((s32[]{:T(128)}, f32[512,8,64]{0,2,1:T(8,128)S(1)}, ...), condition=%wide.region_2.2_spmd.clone, body=%wide.region_1.1_spmd.clone.sunk | while | flops 552339456 | bytes 4204731 | solution.py:61
  (295 shorter events, 197.8 us)
Async XLA Ops:
  7.2 456.8 %reduce-scatter.2.cloned.1.call-start = ((), (), s32[]{:S(2)}) async-start(), calls=%async_computation.1 | async-start | bytes 442368 | tf_op jit(solution)/shard_map/reduce_scatter | solution.py:206
  55.3 9.6 %collective-permute-start.1 = (bf16[128,1024]{1,0:T(8,128)(2,1)}, bf16[128,1024]{1,0:T(8,128)(2,1)S(1)}, u32[]{:S(2)}, u32[]{:S(2)}) collective-permute-start(bf16[128,1024]{1,0:T(8,128)(2,1)} %get-tuple-element.808), channel_id=1, source_target_pairs={{15,0},{0,1},{1,2},{2,3},{3,4},{4,5},{5,6},{6,7},{7,8},{8,9},{9,10... | collective-permute-start | bytes 786440 | tf_op jit(solution)/shard_map/while/body/eval_jaxpr/ppermute | solution.py:15
  66.0 9.7 %collective-permute-start.1 = (bf16[128,1024]{1,0:T(8,128)(2,1)}, bf16[128,1024]{1,0:T(8,128)(2,1)S(1)}, u32[]{:S(2)}, u32[]{:S(2)}) collective-permute-start(bf16[128,1024]{1,0:T(8,128)(2,1)} %get-tuple-element.808), channel_id=1, source_target_pairs={{15,0},{0,1},{1,2},{2,3},{3,4},{4,5},{5,6},{6,7},{7,8},{8,9},{9,10... | collective-permute-start | bytes 786440 | tf_op jit(solution)/shard_map/while/body/eval_jaxpr/ppermute | solution.py:15
  76.8 9.7 %collective-permute-start.1 = (bf16[128,1024]{1,0:T(8,128)(2,1)}, bf16[128,1024]{1,0:T(8,128)(2,1)S(1)}, u32[]{:S(2)}, u32[]{:S(2)}) collective-permute-start(bf16[128,1024]{1,0:T(8,128)(2,1)} %get-tuple-element.808), channel_id=1, source_target_pairs={{15,0},{0,1},{1,2},{2,3},{3,4},{4,5},{5,6},{6,7},{7,8},{8,9},{9,10... | collective-permute-start | bytes 786440 | tf_op jit(solution)/shard_map/while/body/eval_jaxpr/ppermute | solution.py:15
  87.5 9.7 %collective-permute-start.1 = (bf16[128,1024]{1,0:T(8,128)(2,1)}, bf16[128,1024]{1,0:T(8,128)(2,1)S(1)}, u32[]{:S(2)}, u32[]{:S(2)}) collective-permute-start(bf16[128,1024]{1,0:T(8,128)(2,1)} %get-tuple-element.808), channel_id=1, source_target_pairs={{15,0},{0,1},{1,2},{2,3},{3,4},{4,5},{5,6},{6,7},{7,8},{8,9},{9,10... | collective-permute-start | bytes 786440 | tf_op jit(solution)/shard_map/while/body/eval_jaxpr/ppermute | solution.py:15
  98.3 9.7 %collective-permute-start.1 = (bf16[128,1024]{1,0:T(8,128)(2,1)}, bf16[128,1024]{1,0:T(8,128)(2,1)S(1)}, u32[]{:S(2)}, u32[]{:S(2)}) collective-permute-start(bf16[128,1024]{1,0:T(8,128)(2,1)} %get-tuple-element.808), channel_id=1, source_target_pairs={{15,0},{0,1},{1,2},{2,3},{3,4},{4,5},{5,6},{6,7},{7,8},{8,9},{9,10... | collective-permute-start | bytes 786440 | tf_op jit(solution)/shard_map/while/body/eval_jaxpr/ppermute | solution.py:15
  109.1 9.7 %collective-permute-start.1 = (bf16[128,1024]{1,0:T(8,128)(2,1)}, bf16[128,1024]{1,0:T(8,128)(2,1)S(1)}, u32[]{:S(2)}, u32[]{:S(2)}) collective-permute-start(bf16[128,1024]{1,0:T(8,128)(2,1)} %get-tuple-element.808), channel_id=1, source_target_pairs={{15,0},{0,1},{1,2},{2,3},{3,4},{4,5},{5,6},{6,7},{7,8},{8,9},{9,10... | collective-permute-start | bytes 786440 | tf_op jit(solution)/shard_map/while/body/eval_jaxpr/ppermute | solution.py:15
  119.9 9.7 %collective-permute-start.1 = (bf16[128,1024]{1,0:T(8,128)(2,1)}, bf16[128,1024]{1,0:T(8,128)(2,1)S(1)}, u32[]{:S(2)}, u32[]{:S(2)}) collective-permute-start(bf16[128,1024]{1,0:T(8,128)(2,1)} %get-tuple-element.808), channel_id=1, source_target_pairs={{15,0},{0,1},{1,2},{2,3},{3,4},{4,5},{5,6},{6,7},{7,8},{8,9},{9,10... | collective-permute-start | bytes 786440 | tf_op jit(solution)/shard_map/while/body/eval_jaxpr/ppermute | solution.py:15
  130.6 9.7 %collective-permute-start.1 = (bf16[128,1024]{1,0:T(8,128)(2,1)}, bf16[128,1024]{1,0:T(8,128)(2,1)S(1)}, u32[]{:S(2)}, u32[]{:S(2)}) collective-permute-start(bf16[128,1024]{1,0:T(8,128)(2,1)} %get-tuple-element.808), channel_id=1, source_target_pairs={{15,0},{0,1},{1,2},{2,3},{3,4},{4,5},{5,6},{6,7},{7,8},{8,9},{9,10... | collective-permute-start | bytes 786440 | tf_op jit(solution)/shard_map/while/body/eval_jaxpr/ppermute | solution.py:15
  141.4 9.7 %collective-permute-start.1 = (bf16[128,1024]{1,0:T(8,128)(2,1)}, bf16[128,1024]{1,0:T(8,128)(2,1)S(1)}, u32[]{:S(2)}, u32[]{:S(2)}) collective-permute-start(bf16[128,1024]{1,0:T(8,128)(2,1)} %get-tuple-element.808), channel_id=1, source_target_pairs={{15,0},{0,1},{1,2},{2,3},{3,4},{4,5},{5,6},{6,7},{7,8},{8,9},{9,10... | collective-permute-start | bytes 786440 | tf_op jit(solution)/shard_map/while/body/eval_jaxpr/ppermute | solution.py:15
  152.2 9.7 %collective-permute-start.1 = (bf16[128,1024]{1,0:T(8,128)(2,1)}, bf16[128,1024]{1,0:T(8,128)(2,1)S(1)}, u32[]{:S(2)}, u32[]{:S(2)}) collective-permute-start(bf16[128,1024]{1,0:T(8,128)(2,1)} %get-tuple-element.808), channel_id=1, source_target_pairs={{15,0},{0,1},{1,2},{2,3},{3,4},{4,5},{5,6},{6,7},{7,8},{8,9},{9,10... | collective-permute-start | bytes 786440 | tf_op jit(solution)/shard_map/while/body/eval_jaxpr/ppermute | solution.py:15
  163.0 9.7 %collective-permute-start.1 = (bf16[128,1024]{1,0:T(8,128)(2,1)}, bf16[128,1024]{1,0:T(8,128)(2,1)S(1)}, u32[]{:S(2)}, u32[]{:S(2)}) collective-permute-start(bf16[128,1024]{1,0:T(8,128)(2,1)} %get-tuple-element.808), channel_id=1, source_target_pairs={{15,0},{0,1},{1,2},{2,3},{3,4},{4,5},{5,6},{6,7},{7,8},{8,9},{9,10... | collective-permute-start | bytes 786440 | tf_op jit(solution)/shard_map/while/body/eval_jaxpr/ppermute | solution.py:15
  173.7 9.7 %collective-permute-start.1 = (bf16[128,1024]{1,0:T(8,128)(2,1)}, bf16[128,1024]{1,0:T(8,128)(2,1)S(1)}, u32[]{:S(2)}, u32[]{:S(2)}) collective-permute-start(bf16[128,1024]{1,0:T(8,128)(2,1)} %get-tuple-element.808), channel_id=1, source_target_pairs={{15,0},{0,1},{1,2},{2,3},{3,4},{4,5},{5,6},{6,7},{7,8},{8,9},{9,10... | collective-permute-start | bytes 786440 | tf_op jit(solution)/shard_map/while/body/eval_jaxpr/ppermute | solution.py:15
  184.5 9.7 %collective-permute-start.1 = (bf16[128,1024]{1,0:T(8,128)(2,1)}, bf16[128,1024]{1,0:T(8,128)(2,1)S(1)}, u32[]{:S(2)}, u32[]{:S(2)}) collective-permute-start(bf16[128,1024]{1,0:T(8,128)(2,1)} %get-tuple-element.808), channel_id=1, source_target_pairs={{15,0},{0,1},{1,2},{2,3},{3,4},{4,5},{5,6},{6,7},{7,8},{8,9},{9,10... | collective-permute-start | bytes 786440 | tf_op jit(solution)/shard_map/while/body/eval_jaxpr/ppermute | solution.py:15
  195.3 9.7 %collective-permute-start.1 = (bf16[128,1024]{1,0:T(8,128)(2,1)}, bf16[128,1024]{1,0:T(8,128)(2,1)S(1)}, u32[]{:S(2)}, u32[]{:S(2)}) collective-permute-start(bf16[128,1024]{1,0:T(8,128)(2,1)} %get-tuple-element.808), channel_id=1, source_target_pairs={{15,0},{0,1},{1,2},{2,3},{3,4},{4,5},{5,6},{6,7},{7,8},{8,9},{9,10... | collective-permute-start | bytes 786440 | tf_op jit(solution)/shard_map/while/body/eval_jaxpr/ppermute | solution.py:15
  206.1 9.7 %collective-permute-start.1 = (bf16[128,1024]{1,0:T(8,128)(2,1)}, bf16[128,1024]{1,0:T(8,128)(2,1)S(1)}, u32[]{:S(2)}, u32[]{:S(2)}) collective-permute-start(bf16[128,1024]{1,0:T(8,128)(2,1)} %get-tuple-element.808), channel_id=1, source_target_pairs={{15,0},{0,1},{1,2},{2,3},{3,4},{4,5},{5,6},{6,7},{7,8},{8,9},{9,10... | collective-permute-start | bytes 786440 | tf_op jit(solution)/shard_map/while/body/eval_jaxpr/ppermute | solution.py:15
  261.7 9.5 %collective-permute-start = (bf16[128,1024]{1,0:T(8,128)(2,1)S(1)}, bf16[128,1024]{1,0:T(8,128)(2,1)S(1)}, u32[]{:S(2)}, u32[]{:S(2)}) collective-permute-start(bf16[128,1024]{1,0:T(8,128)(2,1)S(1)} %convert_element_type.146), channel_id=1, source_target_pairs={{15,0},{0,1},{1,2},{2,3},{3,4},{4,5},{5,6},{6,7},{7,8},{8,9},{9,10... | collective-permute-start | bytes 786440 | tf_op jit(solution)/shard_map/while/body/eval_jaxpr/ppermute | solution.py:15
  271.3 9.5 %collective-permute-start = (bf16[128,1024]{1,0:T(8,128)(2,1)S(1)}, bf16[128,1024]{1,0:T(8,128)(2,1)S(1)}, u32[]{:S(2)}, u32[]{:S(2)}) collective-permute-start(bf16[128,1024]{1,0:T(8,128)(2,1)S(1)} %convert_element_type.146), channel_id=1, source_target_pairs={{15,0},{0,1},{1,2},{2,3},{3,4},{4,5},{5,6},{6,7},{7,8},{8,9},{9,10... | collective-permute-start | bytes 786440 | tf_op jit(solution)/shard_map/while/body/eval_jaxpr/ppermute | solution.py:15
  280.9 9.5 %collective-permute-start = (bf16[128,1024]{1,0:T(8,128)(2,1)S(1)}, bf16[128,1024]{1,0:T(8,128)(2,1)S(1)}, u32[]{:S(2)}, u32[]{:S(2)}) collective-permute-start(bf16[128,1024]{1,0:T(8,128)(2,1)S(1)} %convert_element_type.146), channel_id=1, source_target_pairs={{15,0},{0,1},{1,2},{2,3},{3,4},{4,5},{5,6},{6,7},{7,8},{8,9},{9,10... | collective-permute-start | bytes 786440 | tf_op jit(solution)/shard_map/while/body/eval_jaxpr/ppermute | solution.py:15
  290.6 9.5 %collective-permute-start = (bf16[128,1024]{1,0:T(8,128)(2,1)S(1)}, bf16[128,1024]{1,0:T(8,128)(2,1)S(1)}, u32[]{:S(2)}, u32[]{:S(2)}) collective-permute-start(bf16[128,1024]{1,0:T(8,128)(2,1)S(1)} %convert_element_type.146), channel_id=1, source_target_pairs={{15,0},{0,1},{1,2},{2,3},{3,4},{4,5},{5,6},{6,7},{7,8},{8,9},{9,10... | collective-permute-start | bytes 786440 | tf_op jit(solution)/shard_map/while/body/eval_jaxpr/ppermute | solution.py:15
  300.2 9.5 %collective-permute-start = (bf16[128,1024]{1,0:T(8,128)(2,1)S(1)}, bf16[128,1024]{1,0:T(8,128)(2,1)S(1)}, u32[]{:S(2)}, u32[]{:S(2)}) collective-permute-start(bf16[128,1024]{1,0:T(8,128)(2,1)S(1)} %convert_element_type.146), channel_id=1, source_target_pairs={{15,0},{0,1},{1,2},{2,3},{3,4},{4,5},{5,6},{6,7},{7,8},{8,9},{9,10... | collective-permute-start | bytes 786440 | tf_op jit(solution)/shard_map/while/body/eval_jaxpr/ppermute | solution.py:15
  309.8 9.5 %collective-permute-start = (bf16[128,1024]{1,0:T(8,128)(2,1)S(1)}, bf16[128,1024]{1,0:T(8,128)(2,1)S(1)}, u32[]{:S(2)}, u32[]{:S(2)}) collective-permute-start(bf16[128,1024]{1,0:T(8,128)(2,1)S(1)} %convert_element_type.146), channel_id=1, source_target_pairs={{15,0},{0,1},{1,2},{2,3},{3,4},{4,5},{5,6},{6,7},{7,8},{8,9},{9,10... | collective-permute-start | bytes 786440 | tf_op jit(solution)/shard_map/while/body/eval_jaxpr/ppermute | solution.py:15
  319.4 9.5 %collective-permute-start = (bf16[128,1024]{1,0:T(8,128)(2,1)S(1)}, bf16[128,1024]{1,0:T(8,128)(2,1)S(1)}, u32[]{:S(2)}, u32[]{:S(2)}) collective-permute-start(bf16[128,1024]{1,0:T(8,128)(2,1)S(1)} %convert_element_type.146), channel_id=1, source_target_pairs={{15,0},{0,1},{1,2},{2,3},{3,4},{4,5},{5,6},{6,7},{7,8},{8,9},{9,10... | collective-permute-start | bytes 786440 | tf_op jit(solution)/shard_map/while/body/eval_jaxpr/ppermute | solution.py:15
  329.0 9.5 %collective-permute-start = (bf16[128,1024]{1,0:T(8,128)(2,1)S(1)}, bf16[128,1024]{1,0:T(8,128)(2,1)S(1)}, u32[]{:S(2)}, u32[]{:S(2)}) collective-permute-start(bf16[128,1024]{1,0:T(8,128)(2,1)S(1)} %convert_element_type.146), channel_id=1, source_target_pairs={{15,0},{0,1},{1,2},{2,3},{3,4},{4,5},{5,6},{6,7},{7,8},{8,9},{9,10... | collective-permute-start | bytes 786440 | tf_op jit(solution)/shard_map/while/body/eval_jaxpr/ppermute | solution.py:15
  338.6 9.5 %collective-permute-start = (bf16[128,1024]{1,0:T(8,128)(2,1)S(1)}, bf16[128,1024]{1,0:T(8,128)(2,1)S(1)}, u32[]{:S(2)}, u32[]{:S(2)}) collective-permute-start(bf16[128,1024]{1,0:T(8,128)(2,1)S(1)} %convert_element_type.146), channel_id=1, source_target_pairs={{15,0},{0,1},{1,2},{2,3},{3,4},{4,5},{5,6},{6,7},{7,8},{8,9},{9,10... | collective-permute-start | bytes 786440 | tf_op jit(solution)/shard_map/while/body/eval_jaxpr/ppermute | solution.py:15
  348.2 9.5 %collective-permute-start = (bf16[128,1024]{1,0:T(8,128)(2,1)S(1)}, bf16[128,1024]{1,0:T(8,128)(2,1)S(1)}, u32[]{:S(2)}, u32[]{:S(2)}) collective-permute-start(bf16[128,1024]{1,0:T(8,128)(2,1)S(1)} %convert_element_type.146), channel_id=1, source_target_pairs={{15,0},{0,1},{1,2},{2,3},{3,4},{4,5},{5,6},{6,7},{7,8},{8,9},{9,10... | collective-permute-start | bytes 786440 | tf_op jit(solution)/shard_map/while/body/eval_jaxpr/ppermute | solution.py:15
  357.8 9.5 %collective-permute-start = (bf16[128,1024]{1,0:T(8,128)(2,1)S(1)}, bf16[128,1024]{1,0:T(8,128)(2,1)S(1)}, u32[]{:S(2)}, u32[]{:S(2)}) collective-permute-start(bf16[128,1024]{1,0:T(8,128)(2,1)S(1)} %convert_element_type.146), channel_id=1, source_target_pairs={{15,0},{0,1},{1,2},{2,3},{3,4},{4,5},{5,6},{6,7},{7,8},{8,9},{9,10... | collective-permute-start | bytes 786440 | tf_op jit(solution)/shard_map/while/body/eval_jaxpr/ppermute | solution.py:15
  367.4 9.5 %collective-permute-start = (bf16[128,1024]{1,0:T(8,128)(2,1)S(1)}, bf16[128,1024]{1,0:T(8,128)(2,1)S(1)}, u32[]{:S(2)}, u32[]{:S(2)}) collective-permute-start(bf16[128,1024]{1,0:T(8,128)(2,1)S(1)} %convert_element_type.146), channel_id=1, source_target_pairs={{15,0},{0,1},{1,2},{2,3},{3,4},{4,5},{5,6},{6,7},{7,8},{8,9},{9,10... | collective-permute-start | bytes 786440 | tf_op jit(solution)/shard_map/while/body/eval_jaxpr/ppermute | solution.py:15
  377.0 9.5 %collective-permute-start = (bf16[128,1024]{1,0:T(8,128)(2,1)S(1)}, bf16[128,1024]{1,0:T(8,128)(2,1)S(1)}, u32[]{:S(2)}, u32[]{:S(2)}) collective-permute-start(bf16[128,1024]{1,0:T(8,128)(2,1)S(1)} %convert_element_type.146), channel_id=1, source_target_pairs={{15,0},{0,1},{1,2},{2,3},{3,4},{4,5},{5,6},{6,7},{7,8},{8,9},{9,10... | collective-permute-start | bytes 786440 | tf_op jit(solution)/shard_map/while/body/eval_jaxpr/ppermute | solution.py:15
  386.6 9.5 %collective-permute-start = (bf16[128,1024]{1,0:T(8,128)(2,1)S(1)}, bf16[128,1024]{1,0:T(8,128)(2,1)S(1)}, u32[]{:S(2)}, u32[]{:S(2)}) collective-permute-start(bf16[128,1024]{1,0:T(8,128)(2,1)S(1)} %convert_element_type.146), channel_id=1, source_target_pairs={{15,0},{0,1},{1,2},{2,3},{3,4},{4,5},{5,6},{6,7},{7,8},{8,9},{9,10... | collective-permute-start | bytes 786440 | tf_op jit(solution)/shard_map/while/body/eval_jaxpr/ppermute | solution.py:15
  396.2 9.5 %collective-permute-start = (bf16[128,1024]{1,0:T(8,128)(2,1)S(1)}, bf16[128,1024]{1,0:T(8,128)(2,1)S(1)}, u32[]{:S(2)}, u32[]{:S(2)}) collective-permute-start(bf16[128,1024]{1,0:T(8,128)(2,1)S(1)} %convert_element_type.146), channel_id=1, source_target_pairs={{15,0},{0,1},{1,2},{2,3},{3,4},{4,5},{5,6},{6,7},{7,8},{8,9},{9,10... | collective-permute-start | bytes 786440 | tf_op jit(solution)/shard_map/while/body/eval_jaxpr/ppermute | solution.py:15
  405.9 9.5 %collective-permute-start = (bf16[128,1024]{1,0:T(8,128)(2,1)S(1)}, bf16[128,1024]{1,0:T(8,128)(2,1)S(1)}, u32[]{:S(2)}, u32[]{:S(2)}) collective-permute-start(bf16[128,1024]{1,0:T(8,128)(2,1)S(1)} %convert_element_type.146), channel_id=1, source_target_pairs={{15,0},{0,1},{1,2},{2,3},{3,4},{4,5},{5,6},{6,7},{7,8},{8,9},{9,10... | collective-permute-start | bytes 786440 | tf_op jit(solution)/shard_map/while/body/eval_jaxpr/ppermute | solution.py:15
  (31 other events, 557.5 us)
Sparse Core Ops, SparseCore 0:
  421.2 33.1 reduce-scatter.1
where the time goes:
time: 474 us; the launch traced here: 472 us
  waiting for transfers between devices  262 us (55%)
  local copies, waits for them, and re-layouts  54.7 us (12%)
  other arithmetic  53.8 us (11%)
  matrix products  51.6 us (11%)
  blocking collectives  30.1 us (6%)
  between operations  15.1 us (3%)
    ppermute x31, waiting for transfers between devices, from_behind(): return lax.ppermute(block, axis, route)  262 us
    reduce_sum x16, other arithmetic, slot_terms(): return jnp.sum(jnp.where(matched[:, None, None], grad_slots, 0.0), 0)  31.2 us
    all_gather x1, blocking collectives, local(): lax.all_gather(item_table, 'item', axis=1, tiled=True)  30.1 us
    dot_general x3, matrix products, key_block(): jnp.einsum('hqk,khd->qhd', weights, v_tile, preferred_element_type=jnp.fl...  14 us
    while x15, local copies, waits for them, and re-layouts  10.5 us
  transfers between devices with their start and end apart: 32, of which 31 were waited for; matrix products, arithmetic and copies ran while one was open for 16% of the time, Pallas kernels for 0%

commit v1 on v0

v1 whole, which is shorter than its diff:
```python
import functools

import jax
import jax.numpy as jnp
from jax import lax
from jax.experimental import pallas as pl
from jax.experimental.pallas import tpu as pltpu
from jax.sharding import PartitionSpec as P

H = 8
GROUP = 4
NORM_EPS = 1e-05
QB = 256
MESH = pl.DeviceIdType.MESH

F32 = jnp.float32
BF16 = jnp.bfloat16


def nn(a, b):
    return lax.dot_general(a, b, (((1,), (0,)), ((), ())), preferred_element_type=F32)


def nt(a, b):
    return lax.dot_general(a, b, (((1,), (1,)), ((), ())), preferred_element_type=F32)


def tn(a, b):
    return lax.dot_general(a, b, (((0,), (0,)), ((), ())), preferred_element_type=F32)


def silu(v):
    half = 0.5 * v
    return half + half * jnp.tanh(half)


def silu_slope(v):
    half = 0.5 * v
    sig = 0.5 + 0.5 * jnp.tanh(half)
    return sig + (v * sig) * (1.0 - sig)


def head_lane(shape, h):
    lane = lax.broadcasted_iota(jnp.int32, shape, len(shape) - 1)
    width = shape[-1] // GROUP
    return (lane >= h * width) & (lane < (h + 1) * width)


def only_head(x, h):
    return jnp.where(head_lane(x.shape, h), x, jnp.zeros_like(x))


def stacked_heads(x):
    return jnp.concatenate([only_head(x, h) for h in range(GROUP)], 0)


def unstacked_heads(x):
    rows = x.shape[0] // GROUP
    total = only_head(x[:rows], 0)
    for h in range(1, GROUP):
        total = total + only_head(x[h * rows : (h + 1) * rows], h)
    return total


def kernel(
    len_ref, lists_ref, ids_ref, table_ref, hist_hbm, win_hbm, wout_hbm, gcand_hbm,
    hist_out, cand_out, tgrad_out,
    hist, win, wout, gcand,
    tab, ids, table, u2, q2, k2, v2, att, outv,
    emb, pre_own, pre_slot, uc, qc, gmix, gatt, wts, slope, gq, gkv, gown,
    contrib, send_back, recv_back, gsend, grecv, coutv, tgv,
    local_sem, out_sem, tab_send, tab_recv, ids_send, ids_recv,
    emb_send, emb_recv, back_send, back_recv, fin_send, fin_recv,
):
    n_item = lax.axis_size("item")
    n_user = lax.axis_size("user")
    me_i = lax.axis_index("item")
    me_u = lax.axis_index("user")
    rows, d = hist.shape
    cand = gcand.shape[0]
    vb, piece = table_ref.shape
    half_vb = vb // 2
    half_cand = cand // 2
    gw = d // 2
    n_slot = contrib.shape[0] - 1
    n_key = k2.shape[1]
    scale = (d // H) ** (-0.5)
    barrier = pltpu.get_barrier_semaphore()

    copies = [
        pltpu.make_async_copy(hist_hbm, hist, local_sem.at[0]),
        pltpu.make_async_copy(win_hbm, win, local_sem.at[1]),
        pltpu.make_async_copy(gcand_hbm, gcand, local_sem.at[2]),
        pltpu.make_async_copy(wout_hbm, wout, local_sem.at[3]),
    ]
    for c in copies:
        c.start()

    def peer_i(k):
        return {"item": lax.rem(me_i + k, n_item)}

    def peer_u(k):
        return {"user": lax.rem(me_u + k, n_user)}

    @pl.loop(1, n_item)
    def _(k):
        pl.semaphore_signal(barrier, inc=1, device_id=peer_i(k), device_id_type=MESH)

    @pl.loop(1, n_user)
    def _(k):
        pl.semaphore_signal(barrier, inc=1, device_id=peer_u(k), device_id_type=MESH)

    tab[me_i] = jnp.concatenate([table_ref[:half_vb], table_ref[half_vb:]], 1)
    ids[me_i] = jnp.broadcast_to(ids_ref[...], ids.shape[1:])
    pl.semaphore_wait(barrier, n_item + n_user - 2)

    def tab_copy(k):
        return pltpu.make_async_remote_copy(
            src_ref=tab.at[me_i], dst_ref=tab.at[me_i], send_sem=tab_send.at[k],
            recv_sem=tab_recv.at[k], device_id=peer_i(k), device_id_type=MESH)

    def ids_copy(k):
        return pltpu.make_async_remote_copy(
            src_ref=ids.at[me_i], dst_ref=ids.at[me_i], send_sem=ids_send.at[k],
            recv_sem=ids_recv.at[k], device_id=peer_i(k), device_id_type=MESH)

    def emb_copy(k):
        return pltpu.make_async_remote_copy(
            src_ref=emb.at[me_u], dst_ref=emb.at[me_u], send_sem=emb_send.at[k],
            recv_sem=emb_recv.at[k], device_id=peer_u(k), device_id_type=MESH)

    def back_copy(k):
        return pltpu.make_async_remote_copy(
            src_ref=send_back.at[k], dst_ref=recv_back.at[k], send_sem=back_send.at[k],
            recv_sem=back_recv.at[k], device_id=peer_u(k), device_id_type=MESH)

    def fin_copy(k):
        return pltpu.make_async_remote_copy(
            src_ref=gsend.at[lax.rem(me_i + k, n_item)], dst_ref=grecv.at[me_i],
            send_sem=fin_send.at[k], recv_sem=fin_recv.at[k],
            device_id=peer_i(k), device_id_type=MESH)

    @pl.loop(1, n_item)
    def _(k):
        tab_copy(k).start()
        ids_copy(k).start()

    length = len_ref[0]
    copies[0].wait()
    copies[1].wait()

    @pl.loop(0, rows // QB)
    def _(b):
        at = pl.ds(pl.multiple_of(b * QB, QB), QB)
        x = hist[at]
        keep = (b * QB + lax.broadcasted_iota(jnp.int32, (QB, 1), 0)) < length
        for g in range(2):
            c = g * gw
            u2[g, at] = silu(nn(x, win[:, c : c + gw])).astype(BF16)
            val = silu(nn(x, win[:, d + c : d + c + gw]))
            v2[g, at] = jnp.where(keep, val, 0.0).astype(BF16)
            q2[g, at] = silu(nn(x, win[:, 2 * d + c : 2 * d + c + gw])).astype(BF16) * (scale / 2)
            k2[g, at] = silu(nn(x, win[:, 3 * d + c : 3 * d + c + gw])).astype(BF16)

    @pl.loop(1, n_item)
    def _(k):
        tab_copy(k).wait_recv()
        ids_copy(k).wait_recv()

    for j in range(tab.shape[0]):
        t = tab[j]
        table[:half_vb, j * piece : (j + 1) * piece] = t[:, :piece]
        table[half_vb:, j * piece : (j + 1) * piece] = t[:, piece:]

    def hot(ids_row):
        row = lax.broadcasted_iota(jnp.int32, (vb, cand), 0)
        return jnp.where(row == ids_row, 1.0, 0.0).astype(BF16)

    own = tn(hot(ids_ref[...]), table[...]).astype(BF16)
    emb[me_u] = own

    @pl.loop(1, n_user)
    def _(k):
        emb_copy(k).start()

    copies[2].wait()
    copies[3].wait()

    pre_own[...] = nn(own, win[...])
    for g in range(2):
        c = g * gw
        uc[g] = silu(pre_own[:, c : c + gw]).astype(BF16)
        v2[g, rows : rows + cand] = silu(pre_own[:, d + c : d + c + gw]).astype(BF16)
        qc[g] = silu(pre_own[:, 2 * d + c : 2 * d + c + gw]).astype(BF16) * (scale / 2)
        k2[g, rows : rows + cand] = silu(pre_own[:, 3 * d + c : 3 * d + c + gw]).astype(BF16)
    gmix[...] = nt(gcand[...], wout[...])

    def normalize(a0, a1):
        mean = (jnp.sum(a0, 1, keepdims=True) + jnp.sum(a1, 1, keepdims=True)) / d
        a0 = a0 - mean
        a1 = a1 - mean
        var = (jnp.sum(a0 * a0, 1, keepdims=True) + jnp.sum(a1 * a1, 1, keepdims=True)) / d
        inv = lax.rsqrt(var + NORM_EPS)
        return a0 * inv, a1 * inv, inv

    def history_block(b):
        lo = b * QB
        n = lo + QB

        @pl.loop(0, 2)
        def _(g):
            q = q2[g, lo:n]
            key = k2[g, :n]
            val = v2[g, :n]
            total = jnp.zeros((QB, gw), F32)
            for h in range(GROUP):
                y = nt(only_head(q, h), key)
                w = y + y * jnp.tanh(y)
                last = w[:, lo:]
                r = lax.broadcasted_iota(jnp.int32, (QB, QB), 0)
                c = lax.broadcasted_iota(jnp.int32, (QB, QB), 1)
                last = jnp.where(c <= r, last, 0.0).astype(BF16)
                if b:
                    w = jnp.concatenate([w[:, :lo].astype(BF16), last], 1)
                else:
                    w = last
                total = total + only_head(nn(w, val), h)
            att[g] = total

        n0, n1, _ = normalize(att[0], att[1])
        m0 = (n0 * u2[0, lo:n].astype(F32)).astype(BF16)
        m1 = (n1 * u2[1, lo:n].astype(F32)).astype(BF16)
        out = nn(m0, wout[:gw]) + nn(m1, wout[gw:]) + hist[lo:n].astype(F32)
        keep = (lo + lax.broadcasted_iota(jnp.int32, (QB, 1), 0)) < length
        outv[lo:n] = jnp.where(keep, out, 0.0).astype(BF16)
        copy = pltpu.make_async_copy(
            outv.at[pl.ds(lo, QB)], hist_out.at[pl.ds(lo, QB)], out_sem.at[b])
        copy.start()
        return copy

    outs = [history_block(3), history_block(0)]

    @pl.loop(1, n_user)
    def _(k):
        emb_copy(k).wait_recv()

    @pl.loop(0, n_slot)
    def _(t):
        e = emb[lists_ref[t]]
        at = pl.ds(pl.multiple_of(rows + cand + t * cand, cand), cand)
        for g in range(2):
            c = g * gw
            pv = nn(e, win[:, d + c : d + c + gw])
            pk = nn(e, win[:, 3 * d + c : 3 * d + c + gw])
            pre_slot[t, :, c : c + gw] = pv
            pre_slot[t, :, d + c : d + c + gw] = pk
            v2[g, at] = silu(pv).astype(BF16)
            k2[g, at] = silu(pk).astype(BF16)

    @pl.loop(0, 2)
    def _(g):
        y = nt(stacked_heads(qc[g]), k2[g])
        t = jnp.tanh(y)
        w = y + y * t
        p = 0.5 + 0.5 * t
        slope[g] = p + w * (1.0 - p)
        wb = w.astype(BF16)
        wts[g] = wb
        att[g, :cand] = unstacked_heads(nn(wb, v2[g]))

    n0, n1, inv = normalize(att[0, :cand], att[1, :cand])
    uc0 = uc[0].astype(F32)
    uc1 = uc[1].astype(F32)
    m0 = (n0 * uc0).astype(BF16)
    m1 = (n1 * uc1).astype(BF16)
    coutv[...] = (nn(m0, wout[:gw]) + nn(m1, wout[gw:]) + own.astype(F32)).astype(BF16)
    cout_copy = pltpu.make_async_copy(coutv, cand_out, out_sem.at[4])
    cout_copy.start()
    gm0 = gmix[:, :gw]
    gm1 = gmix[:, gw:]
    gn0 = gm0 * uc0
    gn1 = gm1 * uc1
    mean_g = (jnp.sum(gn0, 1, keepdims=True) + jnp.sum(gn1, 1, keepdims=True)) / d
    mean_gn = (jnp.sum(gn0 * n0, 1, keepdims=True) + jnp.sum(gn1 * n1, 1, keepdims=True)) / d
    gatt[0] = (inv * (gn0 - mean_g - n0 * mean_gn)).astype(BF16)
    gatt[1] = (inv * (gn1 - mean_g - n1 * mean_gn)).astype(BF16)
    gmix[:, :gw] = gm0 * n0
    gmix[:, gw:] = gm1 * n1

    @pl.loop(0, 2)
    def _(g):
        ga = stacked_heads(gatt[g])
        gwt = nt(ga, v2[g])
        gs = (gwt * slope[g] * scale).astype(BF16)
        gq[g] = unstacked_heads(nn(gs, k2[g]))
        gkv[0, g] = tn(gs[:, rows:], stacked_heads(qc[g])) * (2.0 / scale)
        gkv[1, g] = tn(wts[g, :, rows:], ga)

    @pl.loop(0, n_slot)
    def _(t):
        at = pl.ds(pl.multiple_of(cand + t * cand, cand), cand)
        total = jnp.zeros((cand, d), F32)
        for g in range(2):
            c = g * gw
            dk = (gkv[0, g, at] * silu_slope(pre_slot[t, :, d + c : d + c + gw])).astype(BF16)
            dv = (gkv[1, g, at] * silu_slope(pre_slot[t, :, c : c + gw])).astype(BF16)
            total = total + nt(dv, win[:, d + c : d + c + gw])
            total = total + nt(dk, win[:, 3 * d + c : 3 * d + c + gw])
        contrib[t] = total.astype(BF16)

    contrib[n_slot] = jnp.zeros((cand, d), BF16)

    @pl.loop(1, n_user)
    def _(k):
        owner = lax.rem(me_u + k, n_user)
        slot = n_slot
        for t in range(n_slot):
            slot = jnp.where(lists_ref[t] == owner, t, slot)
        send_back[k] = contrib[slot]
        back_copy(k).start()

    total = gcand[...].astype(F32)
    for g in range(2):
        c = g * gw
        for part, grad in (
            (0, gmix[:, c : c + gw]),
            (1, gkv[1, g, :cand]),
            (2, gq[g]),
            (3, gkv[0, g, :cand]),
        ):
            col = part * d + c
            dp = (grad * silu_slope(pre_own[:, col : col + gw])).astype(BF16)
            total = total + nt(dp, win[:, col : col + gw])
    gown[...] = total

    outs += [history_block(2), history_block(1)]

    @pl.loop(1, n_user)
    def _(k):
        back_copy(k).wait_recv()
        gown[...] += recv_back[k].astype(F32)

    g_all = gown[...].astype(BF16)
    for j in range(tab.shape[0]):
        x = g_all[:, j * piece : (j + 1) * piece]
        gsend[j] = jnp.concatenate([x[:half_cand], x[half_cand:]], 1)
    grecv[me_i] = gsend[me_i]

    @pl.loop(1, n_item)
    def _(k):
        fin_copy(k).start()

    @pl.loop(1, n_item)
    def _(k):
        fin_copy(k).wait_recv()

    tg = jnp.zeros((vb, piece), F32)
    for j in range(tab.shape[0]):
        x = grecv[j]
        x = jnp.concatenate([x[:, :piece], x[:, piece:]], 0)
        tg = tg + nn(hot(ids[j, :1]), x)
    tgv[...] = tg
    tg_copy = pltpu.make_async_copy(tgv, tgrad_out, out_sem.at[5])
    tg_copy.start()

    @pl.loop(1, n_item)
    def _(k):
        tab_copy(k).wait_send()
        ids_copy(k).wait_send()
        fin_copy(k).wait_send()

    @pl.loop(1, n_user)
    def _(k):
        emb_copy(k).wait_send()
        back_copy(k).wait_send()

    for c in outs:
        c.wait()
    cout_copy.wait()
    tg_copy.wait()


def local(history, hist_len, cand_ids, cand_lists, item_table, w_in, w_out, grad_cand):
    rows, d = history.shape[1:]
    cand = cand_ids.shape[1]
    n_slot = cand_lists.shape[1]
    vb, piece = item_table.shape
    n_item = lax.axis_size("item")
    n_user = lax.axis_size("user")
    gw = d // 2
    n_key = rows + (1 + n_slot) * cand
    vmem = pl.BlockSpec(memory_space=pltpu.VMEM)
    smem = pl.BlockSpec(memory_space=pltpu.SMEM)
    hbm = pl.BlockSpec(memory_space=pl.ANY)
    V = pltpu.VMEM
    dma = pltpu.SemaphoreType.DMA
    hist_out, cand_out, tgrad = pl.pallas_call(
        kernel,
        out_shape=(
            jax.ShapeDtypeStruct((rows, d), BF16),
            jax.ShapeDtypeStruct((cand, d), BF16),
            jax.ShapeDtypeStruct((vb, piece), F32),
        ),
        in_specs=[smem, smem, vmem, vmem, hbm, hbm, hbm, hbm],
        out_specs=(hbm, hbm, hbm),
        scratch_shapes=[
            V((rows, d), BF16), V((d, 4 * d), BF16), V((d, d), BF16), V((cand, d), BF16),
            V((n_item, vb // 2, 2 * piece), BF16), V((n_item, 8, cand), jnp.int32),
            V((vb, d), BF16),
            V((2, rows, gw), BF16), V((2, rows, gw), BF16),
            V((2, n_key, gw), BF16), V((2, n_key, gw), BF16),
            V((2, QB, gw), F32), V((rows, d), BF16),
            V((n_user, cand, d), BF16), V((cand, 4 * d), F32), V((n_slot, cand, 2 * d), F32),
            V((2, cand, gw), BF16), V((2, cand, gw), BF16), V((cand, d), F32),
            V((2, cand, gw), BF16),
            V((2, GROUP * cand, n_key), BF16), V((2, GROUP * cand, n_key), F32),
            V((2, cand, gw), F32), V((2, 2, (1 + n_slot) * cand, gw), F32), V((cand, d), F32),
            V((n_slot + 1, cand, d), BF16), V((n_user, cand, d), BF16),
            V((n_user, cand, d), BF16),
            V((n_item, cand // 2, 2 * piece), BF16), V((n_item, cand // 2, 2 * piece), BF16),
            V((cand, d), BF16), V((vb, piece), F32),
            dma((4,)), dma((6,)),
            dma((n_item,)), dma((n_item,)), dma((n_item,)), dma((n_item,)),
            dma((n_user,)), dma((n_user,)), dma((n_user,)), dma((n_user,)),
            dma((n_item,)), dma((n_item,)),
        ],
        compiler_params=pltpu.CompilerParams(
            collective_id=0, has_side_effects=True, vmem_limit_bytes=56 * 1024 * 1024),
    )(
        hist_len, cand_lists[0], cand_ids, item_table, history[0], w_in, w_out, grad_cand[0],
    )
    return hist_out[None], cand_out[None], tgrad


def solution(mesh):
    in_specs = (
        P(("item", "user"), None, None),
        P(("item", "user")),
        P(("item", "user"), None),
        P(("item", "user"), None),
        P("user", "item"),
        P(),
        P(),
        P(("item", "user"), None, None),
    )
    out_specs = (
        P(("item", "user"), None, None),
        P(("item", "user"), None, None),
        P("user", "item"),
    )
    return jax.shard_map(local, mesh=mesh, in_specs=in_specs, out_specs=out_specs, check_vma=False)
```

time: 474 us -> 97.9 us (0.21)
  the two profiles are of different devices: /device:TPU:32 before, /device:TPU:25 now
where the time goes in v1:
time: 97.9 us; the launch traced here: 97.6 us
  Pallas kernels  90.1 us (92%)
  local copies, waits for them, and re-layouts  6.18 us (6%)
  between operations  1.29 us (1%)
    pallas_call x1, Pallas kernels, local(): pl.pallas_call(kernel, out_shape=(jax.ShapeDtypeStruct((rows, d), BF16),...  90.1 us
    unnamed x6, local copies, waits for them, and re-layouts  6.18 us

profile of v1, /device:TPU:25, one launch (start us, length us, event | category | flops | bytes accessed | tf_op | source)
XLA Modules:
  0.0 97.6 jit_solution(17318220500012965359)
XLA Ops:
  1.3 1.5 %copy.11.table_ref = bf16[384,64]{1,0:T(8,128)(2,1)} copy(bf16[384,64]{0,1:T(8,128)(2,1)} %param.12) | data formatting | bytes 98304 | tf_op args[4]
  2.8 90.1 %shard_map.103 = (bf16[1024,512]{1,0:T(8,128)(2,1)}, bf16[128,512]{1,0:T(8,128)(2,1)}, f32[384,64]{1,0:T(8,128)}) custom-call(s32[1]{0:T(128)S(6)} %copy.15.len_ref, s32[4]{0:T(128)} %bitcast.9, s32[1,128]{1,0:T(1,128)} %ids_ref.1, bf16[384,64]{1,0:T(8,128)(2,1)} %copy.11.table_ref, bf16[1024,512]{1,0:T(8,128)(2,1)} %bitcast.5, bf16[512,2048]{1,0:T(8,128)(2,1)} %win_hbm.1, ...), custom_call_target="tpu_custom_call" | custom-call | tf_op jit(solution)/shard_map/pallas_call | solution.py:397
  93.0 0.0 copy-start
  93.0 1.7 %copy.12 = f32[384,64]{0,1:T(8,128)} copy(f32[384,64]{1,0:T(8,128)} %get-tuple-element.11) | data formatting | bytes 196608
  94.7 2.3 %copy.16 = bf16[1,1024,512]{2,1,0:T(8,128)(2,1)} copy(bf16[1,1024,512]{2,1,0:T(8,128)(2,1)} %bitcast.6) | data formatting | bytes 2097152
  96.9 0.0 copy-done
  97.0 0.7 copy.17
Async XLA Ops:
  93.0 4.0 %copy-start = (bf16[128,512]{1,0:T(8,128)(2,1)S(1)}, bf16[128,512]{1,0:T(8,128)(2,1)}, u32[]{:S(2)}) copy-start(bf16[128,512]{1,0:T(8,128)(2,1)} %get-tuple-element.7) | copy-start | bytes 393220

commit v2 on v1

v2 whole, which is shorter than its diff:
```python
import functools

import jax
import jax.numpy as jnp
from jax import lax
from jax.experimental import pallas as pl
from jax.experimental.pallas import tpu as pltpu
from jax.sharding import PartitionSpec as P

H = 8
GROUP = 4
NORM_EPS = 1e-05
QB = 256
MESH = pl.DeviceIdType.MESH

F32 = jnp.float32
BF16 = jnp.bfloat16


def nn(a, b):
    return lax.dot_general(a, b, (((1,), (0,)), ((), ())), preferred_element_type=F32)


def nt(a, b):
    return lax.dot_general(a, b, (((1,), (1,)), ((), ())), preferred_element_type=F32)


def tn(a, b):
    return lax.dot_general(a, b, (((0,), (0,)), ((), ())), preferred_element_type=F32)


def silu(v):
    half = 0.5 * v
    return half + half * jnp.tanh(half)


def silu_slope(v):
    half = 0.5 * v
    sig = 0.5 + 0.5 * jnp.tanh(half)
    return sig + (v * sig) * (1.0 - sig)


def head_lane(shape, h):
    lane = lax.broadcasted_iota(jnp.int32, shape, len(shape) - 1)
    width = shape[-1] // GROUP
    return (lane >= h * width) & (lane < (h + 1) * width)


def only_head(x, h):
    return jnp.where(head_lane(x.shape, h), x, jnp.zeros_like(x))


def stacked_heads(x):
    return jnp.concatenate([only_head(x, h) for h in range(GROUP)], 0)


def unstacked_heads(x):
    rows = x.shape[0] // GROUP
    total = only_head(x[:rows], 0)
    for h in range(1, GROUP):
        total = total + only_head(x[h * rows : (h + 1) * rows], h)
    return total


def kernel(
    len_ref, lists_ref, ids_ref, table_hbm, hist_hbm, win_hbm, wout_hbm, gcand_hbm,
    hist_out, cand_out, tgrad_out, *,
    hist, win, wout, gcand, tabc, tags, tags_i, pick, back, hotc, e_all, disp, eown, eslot,
    u2, q2, k2, v2, att, catt, outv, pre_own, pre_slot, uc, qc, gmix, gatt, wts, slope, gq, gkv,
    dsend, drecv, share, share_in, csum, fin, coutv, tgv,
    local_sem, out_sem, s_tab, r_tab, s_tag, r_tag, s_tagi, r_tagi, s_own, r_own, s_slot, r_slot,
    s_back, r_back, s_share, r_share, s_fin, r_fin,
):
    n_item = lax.axis_size("item")
    n_user = lax.axis_size("user")
    me_i = lax.axis_index("item")
    me_u = lax.axis_index("user")
    rows, d = hist.shape
    cand = gcand.shape[0]
    chunk, vb = tabc.shape[1:]
    piece = table_hbm.shape[0]
    per = piece // chunk
    gw = d // 2
    n_slot = eslot.shape[1] // chunk
    own_end = rows + cand
    scale = (d // H) ** (-0.5)
    barrier = pltpu.get_barrier_semaphore()
    holder = me_u // per
    at_home = holder == me_i

    copies = [
        pltpu.make_async_copy(hist_hbm, hist, local_sem.at[0]),
        pltpu.make_async_copy(win_hbm, win, local_sem.at[1]),
        pltpu.make_async_copy(gcand_hbm, gcand, local_sem.at[2]),
        pltpu.make_async_copy(wout_hbm, wout, local_sem.at[3]),
    ]

    def peer_i(k):
        return {"item": lax.rem(me_i + k, n_item)}

    def peer_u(k):
        return {"user": lax.rem(me_u + k, n_user)}

    def worker(n):
        return (lax.rem(me_i + n // per, n_item), me_i * per + lax.rem(n, per))

    def not_me(place):
        return jnp.logical_or(place[0] != me_i, place[1] != me_u)

    def signal(place):
        pl.semaphore_signal(barrier, inc=1, device_id=place, device_id_type=MESH)

    @pl.loop(1, n_item)
    def _(k):
        signal(peer_i(k))

    @pl.loop(1, n_user)
    def _(k):
        signal(peer_u(k))

    @pl.loop(0, n_user)
    def _(n):
        @pl.when(not_me(worker(n)))
        def _():
            signal(worker(n))

        @pl.when(not_me((holder, n)))
        def _():
            signal((holder, n))

    for c in copies:
        c.start()

    lane = lax.broadcasted_iota(jnp.int32, (1, cand), 1)
    key_row = jnp.zeros((1, cand), jnp.int32)
    for t in range(n_slot):
        key_row = jnp.where(lane // chunk == t, lists_ref[t] * chunk + lane - t * chunk, key_row)
    tag = jnp.concatenate([ids_ref[...], key_row, jnp.zeros((6, cand), jnp.int32)], 0)
    tags[me_u] = tag
    tags_i[me_i] = tag

    def remote(src, dst, send, recv, place):
        return pltpu.make_async_remote_copy(
            src_ref=src, dst_ref=dst, send_sem=send, recv_sem=recv, device_id=place,
            device_id_type=MESH)

    def tag_copy(k):
        return remote(tags.at[me_u], tags.at[me_u], s_tag.at[k], r_tag.at[k], peer_u(k))

    def tagi_copy(k):
        return remote(tags_i.at[me_i], tags_i.at[me_i], s_tagi.at[k], r_tagi.at[k], peer_i(k))

    def tab_copy(n):
        at = pl.ds(pl.multiple_of(lax.rem(n, per) * chunk, chunk), chunk)
        return remote(table_hbm.at[at], tabc.at[me_u], s_tab.at[n], r_tab.at[me_u], worker(n))

    def tab_arrival(u):
        return remote(tabc.at[u], tabc.at[u], s_tab.at[u], r_tab.at[u], (holder, u))

    def own_copy(k):
        to = lax.rem(me_u + k, n_user)
        return remote(e_all.at[to], eown.at[me_u], s_own.at[k], r_own.at[k], peer_u(k))

    def slot_copy(k):
        to = lax.rem(me_u + k, n_user)
        return remote(disp.at[to], eslot.at[me_u], s_slot.at[k], r_slot.at[k], peer_u(k))

    def back_copy(k):
        to = lax.rem(me_u + k, n_user)
        return remote(dsend.at[to], drecv.at[me_u], s_back.at[k], r_back.at[k], peer_u(k))

    def share_copy(k):
        to = lax.rem(me_i + k, n_item)
        return remote(share.at[to], share_in.at[me_i], s_share.at[k], r_share.at[k], peer_i(k))

    def fin_copy(r):
        n = me_i * per + lax.rem(me_u, per)
        return remote(csum.at[r], fin.at[n], s_fin.at[r], r_fin.at[n], (holder, r))

    def fin_arrival(n):
        return remote(fin.at[n], fin.at[n], s_fin.at[n], r_fin.at[n], (n // per, me_i * per + n % per))

    home_at = pl.ds(pl.multiple_of(lax.rem(me_u, per) * chunk, chunk), chunk)
    home_copy = pltpu.make_async_copy(table_hbm.at[home_at], tabc.at[me_u], local_sem.at[4])

    pl.semaphore_wait(
        barrier, n_item + 3 * n_user - 2 - 2 * at_home.astype(jnp.int32))

    @pl.loop(0, n_user)
    def _(n):
        @pl.when(not_me(worker(n)))
        def _():
            tab_copy(n).start()

    @pl.when(at_home)
    def _():
        home_copy.start()

    @pl.loop(1, n_user)
    def _(k):
        tag_copy(k).start()

    @pl.loop(1, n_item)
    def _(k):
        tagi_copy(k).start()

    length = len_ref[0]
    for c in copies:
        c.wait()

    @pl.loop(0, rows // QB)
    def _(b):
        at = pl.ds(pl.multiple_of(b * QB, QB), QB)
        x = hist[at]
        keep = (b * QB + lax.broadcasted_iota(jnp.int32, (QB, 1), 0)) < length
        for g in range(2):
            c = g * gw
            u2[g, at] = silu(nn(x, win[:, c : c + gw])).astype(BF16)
            val = silu(nn(x, win[:, d + c : d + c + gw]))
            v2[g, at] = jnp.where(keep, val, 0.0).astype(BF16)
            q2[g, at] = silu(nn(x, win[:, 2 * d + c : 2 * d + c + gw])).astype(BF16) * (scale / 2)
            k2[g, at] = silu(nn(x, win[:, 3 * d + c : 3 * d + c + gw])).astype(BF16)

    gmix[...] = nt(gcand[...], wout[...])

    @pl.loop(1, n_user)
    def _(k):
        tag_copy(k).wait_recv()

    keys = jnp.concatenate([tags[u, 1:2] for u in range(n_user)], 0)
    keys_t = jnp.transpose(keys.astype(F32)).astype(jnp.int32)
    line = n_slot * chunk
    col = lax.broadcasted_iota(jnp.int32, (line, n_user * chunk), 1)
    row = lax.broadcasted_iota(jnp.int32, (n_user * chunk, line), 0)
    for u in range(n_user):
        pick[u * line : (u + 1) * line] = jnp.where(
            col == keys_t[:, u : u + 1], 1.0, 0.0).astype(BF16)
        back[:, u * line : (u + 1) * line] = jnp.where(
            row == keys[u : u + 1], 1.0, 0.0).astype(BF16)

    @pl.loop(0, n_user)
    def _(u):
        @pl.when(not_me((holder, u)))
        def _():
            tab_arrival(u).wait_recv()

    @pl.when(at_home)
    def _():
        home_copy.wait()

    @pl.loop(0, n_user)
    def _(u):
        at = lax.broadcasted_iota(jnp.int32, (vb, cand), 0)
        hot = jnp.where(at == tags[u, 0:1], 1.0, 0.0).astype(BF16)
        e_all[u] = nn(tabc[u], hot).astype(BF16)

    eown[me_u] = e_all[me_u]

    @pl.loop(1, n_user)
    def _(k):
        own_copy(k).start()

    picked = nn(pick[...], e_all[...].reshape(n_user * chunk, cand)).astype(BF16)
    disp[...] = picked.reshape(disp.shape)
    eslot[me_u] = disp[me_u]

    @pl.loop(1, n_user)
    def _(k):
        slot_copy(k).start()

    def normalize(a0, a1):
        mean = (jnp.sum(a0, 1, keepdims=True) + jnp.sum(a1, 1, keepdims=True)) / d
        a0 = a0 - mean
        a1 = a1 - mean
        var = (jnp.sum(a0 * a0, 1, keepdims=True) + jnp.sum(a1 * a1, 1, keepdims=True)) / d
        inv = lax.rsqrt(var + NORM_EPS)
        return a0 * inv, a1 * inv, inv

    def history_block(b):
        lo = b * QB
        n = lo + QB

        @pl.loop(0, 2)
        def _(g):
            q = q2[g, lo:n]
            key = k2[g, :n]
            val = v2[g, :n]
            total = jnp.zeros((QB, gw), F32)
            for h in range(GROUP):
                y = nt(only_head(q, h), key)
                w = y + y * jnp.tanh(y)
                last = w[:, lo:]
                r = lax.broadcasted_iota(jnp.int32, (QB, QB), 0)
                c = lax.broadcasted_iota(jnp.int32, (QB, QB), 1)
                last = jnp.where(c <= r, last, 0.0).astype(BF16)
                if b:
                    w = jnp.concatenate([w[:, :lo].astype(BF16), last], 1)
                else:
                    w = last
                total = total + only_head(nn(w, val), h)
            att[g] = total

        n0, n1, _ = normalize(att[0], att[1])
        m0 = (n0 * u2[0, lo:n].astype(F32)).astype(BF16)
        m1 = (n1 * u2[1, lo:n].astype(F32)).astype(BF16)
        out = nn(m0, wout[:gw]) + nn(m1, wout[gw:]) + hist[lo:n].astype(F32)
        keep = (lo + lax.broadcasted_iota(jnp.int32, (QB, 1), 0)) < length
        outv[lo:n] = jnp.where(keep, out, 0.0).astype(BF16)
        copy = pltpu.make_async_copy(
            outv.at[pl.ds(lo, QB)], hist_out.at[pl.ds(lo, QB)], out_sem.at[b])
        copy.start()
        return copy

    outs = [history_block(1)]

    @pl.loop(1, n_user)
    def _(k):
        own_copy(k).wait_recv()

    own = jnp.transpose(eown[...].reshape(d, cand).astype(F32)).astype(BF16)
    pre_own[...] = nn(own, win[...])
    for g in range(2):
        c = g * gw
        uc[g] = silu(pre_own[:, c : c + gw]).astype(BF16)
        v2[g, rows:own_end] = silu(pre_own[:, d + c : d + c + gw]).astype(BF16)
        qc[g] = silu(pre_own[:, 2 * d + c : 2 * d + c + gw]).astype(BF16) * (scale / 2)
        k2[g, rows:own_end] = silu(pre_own[:, 3 * d + c : 3 * d + c + gw]).astype(BF16)

    def scores(g, lo, hi):
        y = nt(stacked_heads(qc[g]), k2[g, lo:hi])
        t = jnp.tanh(y)
        w = y + y * t
        p = 0.5 + 0.5 * t
        slope[g, :, lo:hi] = p + w * (1.0 - p)
        wb = w.astype(BF16)
        late = max(lo, rows)
        wts[g, :, late - rows : hi - rows] = wb[:, late - lo :]
        return unstacked_heads(nn(wb, v2[g, lo:hi]))

    @pl.loop(0, 2)
    def _(g):
        catt[g] = scores(g, 0, own_end)

    outs += [history_block(2)]

    @pl.loop(1, n_user)
    def _(k):
        slot_copy(k).wait_recv()

    for t in range(n_slot):
        e = eslot[:, t * chunk : (t + 1) * chunk].reshape(d, cand)
        e = jnp.transpose(e.astype(F32)).astype(BF16)
        at = pl.ds(own_end + t * cand, cand)
        for g in range(2):
            c = g * gw
            pv = nn(e, win[:, d + c : d + c + gw])
            pk = nn(e, win[:, 3 * d + c : 3 * d + c + gw])
            pre_slot[t, :, c : c + gw] = pv
            pre_slot[t, :, d + c : d + c + gw] = pk
            v2[g, at] = silu(pv).astype(BF16)
            k2[g, at] = silu(pk).astype(BF16)

    n_key = k2.shape[1]

    @pl.loop(0, 2)
    def _(g):
        catt[g] += scores(g, own_end, n_key)

    n0, n1, inv = normalize(catt[0], catt[1])
    uc0 = uc[0].astype(F32)
    uc1 = uc[1].astype(F32)
    gm0 = gmix[:, :gw]
    gm1 = gmix[:, gw:]
    gn0 = gm0 * uc0
    gn1 = gm1 * uc1
    mean_g = (jnp.sum(gn0, 1, keepdims=True) + jnp.sum(gn1, 1, keepdims=True)) / d
    mean_gn = (jnp.sum(gn0 * n0, 1, keepdims=True) + jnp.sum(gn1 * n1, 1, keepdims=True)) / d
    gatt[0] = (inv * (gn0 - mean_g - n0 * mean_gn)).astype(BF16)
    gatt[1] = (inv * (gn1 - mean_g - n1 * mean_gn)).astype(BF16)
    gmix[:, :gw] = gm0 * n0
    gmix[:, gw:] = gm1 * n1
    m0 = (n0 * uc0).astype(BF16)
    m1 = (n1 * uc1).astype(BF16)

    def score_grads(g, lo, hi):
        ga = stacked_heads(gatt[g])
        gs = (nt(ga, v2[g, lo:hi]) * slope[g, :, lo:hi] * scale).astype(BF16)
        late = max(lo, rows)
        gkv[0, g, late - rows : hi - rows] = tn(
            gs[:, late - lo :], stacked_heads(qc[g])) * (2.0 / scale)
        gkv[1, g, late - rows : hi - rows] = tn(wts[g, :, late - rows : hi - rows], ga)
        return unstacked_heads(nn(gs, k2[g, lo:hi]))

    @pl.loop(0, 2)
    def _(g):
        gq[g] = score_grads(g, own_end, n_key)

    for t in range(n_slot):
        at = pl.ds(cand + t * cand, cand)
        total = jnp.zeros((d, cand), F32)
        for g in range(2):
            c = g * gw
            dk = (gkv[0, g, at] * silu_slope(pre_slot[t, :, d + c : d + c + gw])).astype(BF16)
            dv = (gkv[1, g, at] * silu_slope(pre_slot[t, :, c : c + gw])).astype(BF16)
            total = total + nt(win[:, d + c : d + c + gw], dv)
            total = total + nt(win[:, 3 * d + c : 3 * d + c + gw], dk)
        dsend[:, t * chunk : (t + 1) * chunk] = total.astype(BF16).reshape(n_user, chunk, cand)

    drecv[me_u] = dsend[me_u]

    @pl.loop(1, n_user)
    def _(k):
        back_copy(k).start()

    coutv[...] = (nn(m0, wout[:gw]) + nn(m1, wout[gw:]) + own.astype(F32)).astype(BF16)
    cout_copy = pltpu.make_async_copy(coutv, cand_out, out_sem.at[4])
    cout_copy.start()

    @pl.loop(0, 2)
    def _(g):
        gq[g] += score_grads(g, 0, own_end)

    total = jnp.transpose(gcand[...].astype(F32))
    for g in range(2):
        c = g * gw
        for part, grad in (
            (0, gmix[:, c : c + gw]),
            (1, gkv[1, g, :cand]),
            (2, gq[g]),
            (3, gkv[0, g, :cand]),
        ):
            cl = part * d + c
            dp = (grad * silu_slope(pre_own[:, cl : cl + gw])).astype(BF16)
            total = total + nt(win[:, cl : cl + gw], dp)
    share[...] = total.astype(BF16).reshape(share.shape)
    share_in[me_i] = share[me_i]

    @pl.loop(1, n_item)
    def _(k):
        share_copy(k).start()

    outs += [history_block(3)]

    @pl.loop(1, n_user)
    def _(k):
        back_copy(k).wait_recv()

    summed = nn(back[...], drecv[...].reshape(n_user * line, cand)).astype(BF16)
    csum[...] = summed.reshape(csum.shape)

    @pl.loop(0, n_user)
    def _(r):
        @pl.when(not_me((holder, r)))
        def _():
            fin_copy(r).start()

    @pl.when(at_home)
    def _():
        fin[me_u] = csum[me_u]

    outs += [history_block(0)]

    @pl.loop(1, n_item)
    def _(k):
        tagi_copy(k).wait_recv()
        share_copy(k).wait_recv()

    ids_t = jnp.concatenate([tags_i[i, 0:1] for i in range(n_item)], 0)
    ids_t = jnp.transpose(ids_t.astype(F32)).astype(jnp.int32)
    col = lax.broadcasted_iota(jnp.int32, (cand, vb), 1)
    tg = jnp.zeros((piece, vb), F32)
    for i in range(n_item):
        hotc[i] = jnp.where(col == ids_t[:, i : i + 1], 1.0, 0.0).astype(BF16)
        tg = tg + nn(share_in[i], hotc[i])
    tgv[...] = tg

    @pl.loop(0, n_user)
    def _(n):
        @pl.when(not_me((n // per, me_i * per + lax.rem(n, per))))
        def _():
            fin_arrival(n).wait_recv()

    tg = tgv[...]
    for i in range(n_item):
        tg = tg + nn(fin[i * per : (i + 1) * per].reshape(piece, cand), hotc[i])
    tgv[...] = tg
    tg_copy = pltpu.make_async_copy(tgv, tgrad_out, out_sem.at[5])
    tg_copy.start()

    @pl.loop(1, n_item)
    def _(k):
        tagi_copy(k).wait_send()
        share_copy(k).wait_send()

    @pl.loop(1, n_user)
    def _(k):
        tag_copy(k).wait_send()
        own_copy(k).wait_send()
        slot_copy(k).wait_send()
        back_copy(k).wait_send()

    @pl.loop(0, n_user)
    def _(n):
        @pl.when(not_me(worker(n)))
        def _():
            tab_copy(n).wait_send()

        @pl.when(not_me((holder, n)))
        def _():
            fin_copy(n).wait_send()

    for c in outs:
        c.wait()
    cout_copy.wait()
    tg_copy.wait()


def local(history, hist_len, cand_ids, cand_lists, item_table, w_in, w_out, grad_cand):
    rows, d = history.shape[1:]
    cand = cand_ids.shape[1]
    n_slot = cand_lists.shape[1]
    vb, piece = item_table.shape
    n_item = lax.axis_size("item")
    n_user = lax.axis_size("user")
    gw = d // 2
    chunk = d // n_user
    n_late = (1 + n_slot) * cand
    n_key = rows + n_late
    vmem = pl.BlockSpec(memory_space=pltpu.VMEM)
    smem = pl.BlockSpec(memory_space=pltpu.SMEM)
    hbm = pl.BlockSpec(memory_space=pl.ANY)
    V = pltpu.VMEM
    dma = pltpu.SemaphoreType.DMA
    scratch = dict(
        hist=V((rows, d), BF16), win=V((d, 4 * d), BF16), wout=V((d, d), BF16),
        gcand=V((cand, d), BF16),
        tabc=V((n_user, chunk, vb), BF16),
        tags=V((n_user, 8, cand), jnp.int32), tags_i=V((n_item, 8, cand), jnp.int32),
        pick=V((n_user * n_slot * chunk, n_user * chunk), BF16),
        back=V((n_user * chunk, n_user * n_slot * chunk), BF16),
        hotc=V((n_item, cand, vb), BF16),
        e_all=V((n_user, chunk, cand), BF16), disp=V((n_user, n_slot * chunk, cand), BF16),
        eown=V((n_user, chunk, cand), BF16), eslot=V((n_user, n_slot * chunk, cand), BF16),
        u2=V((2, rows, gw), BF16), q2=V((2, rows, gw), BF16),
        k2=V((2, n_key, gw), BF16), v2=V((2, n_key, gw), BF16),
        att=V((2, QB, gw), F32), catt=V((2, cand, gw), F32), outv=V((rows, d), BF16),
        pre_own=V((cand, 4 * d), F32), pre_slot=V((n_slot, cand, 2 * d), F32),
        uc=V((2, cand, gw), BF16), qc=V((2, cand, gw), BF16), gmix=V((cand, d), F32),
        gatt=V((2, cand, gw), BF16),
        wts=V((2, GROUP * cand, n_late), BF16), slope=V((2, GROUP * cand, n_key), F32),
        gq=V((2, cand, gw), F32), gkv=V((2, 2, n_late, gw), F32),
        dsend=V((n_user, n_slot * chunk, cand), BF16),
        drecv=V((n_user, n_slot * chunk, cand), BF16),
        share=V((n_item, piece, cand), BF16), share_in=V((n_item, piece, cand), BF16),
        csum=V((n_user, chunk, cand), BF16), fin=V((n_user, chunk, cand), BF16),
        coutv=V((cand, d), BF16), tgv=V((piece, vb), F32),
        local_sem=dma((5,)), out_sem=dma((6,)),
        s_tab=dma((n_user,)), r_tab=dma((n_user,)),
        s_tag=dma((n_user,)), r_tag=dma((n_user,)),
        s_tagi=dma((n_item,)), r_tagi=dma((n_item,)),
        s_own=dma((n_user,)), r_own=dma((n_user,)),
        s_slot=dma((n_user,)), r_slot=dma((n_user,)),
        s_back=dma((n_user,)), r_back=dma((n_user,)),
        s_share=dma((n_item,)), r_share=dma((n_item,)),
        s_fin=dma((n_user,)), r_fin=dma((n_user,)),
    )
    names = list(scratch)

    def body(*refs):
        kernel(*refs[:11], **dict(zip(names, refs[11:])))

    hist_out, cand_out, tgrad = pl.pallas_call(
        body,
        out_shape=(
            jax.ShapeDtypeStruct((rows, d), BF16),
            jax.ShapeDtypeStruct((cand, d), BF16),
            jax.ShapeDtypeStruct((piece, vb), F32),
        ),
        in_specs=[smem, smem, vmem, hbm, hbm, hbm, hbm, hbm],
        out_specs=(hbm, hbm, hbm),
        scratch_shapes=list(scratch.values()),
        compiler_params=pltpu.CompilerParams(
            collective_id=0, has_side_effects=True, vmem_limit_bytes=58 * 1024 * 1024),
    )(
        hist_len, cand_lists[0], cand_ids, item_table.T, history[0], w_in, w_out, grad_cand[0],
    )
    return hist_out[None], cand_out[None], tgrad.T


def solution(mesh):
    in_specs = (
        P(("item", "user"), None, None),
        P(("item", "user")),
        P(("item", "user"), None),
        P(("item", "user"), None),
        P("user", "item"),
        P(),
        P(),
        P(("item", "user"), None, None),
    )
    out_specs = (
        P(("item", "user"), None, None),
        P(("item", "user"), None, None),
        P("user", "item"),
    )
    return jax.shard_map(local, mesh=mesh, in_specs=in_specs, out_specs=out_specs, check_vma=False)
```

time: 97.9 us -> 73.6 us (0.75)
  the two profiles are of different devices: /device:TPU:25 before, /device:TPU:1 now
where the time goes in v2:
time: 73.6 us; the launch traced here: 73.3 us
  Pallas kernels  68.4 us (93%)
  local copies, waits for them, and re-layouts  3.61 us (5%)
  between operations  1.3 us (2%)
    pallas_call x1, Pallas kernels, local(): pl.pallas_call(body, out_shape=(jax.ShapeDtypeStruct((rows, d), BF16), ja...  68.4 us
    unnamed x7, local copies, waits for them, and re-layouts  3.61 us

profile of v2, /device:TPU:1, one launch (start us, length us, event | category | flops | bytes accessed | tf_op | source)
XLA Modules:
  0.0 73.3 jit_solution(772761954939043314)
XLA Ops:
  1.3 68.4 %shard_map.103 = (bf16[1024,512]{1,0:T(8,128)(2,1)}, bf16[128,512]{1,0:T(8,128)(2,1)}, f32[64,384]{1,0:T(8,128)}) custom-call(s32[1]{0:T(128)S(6)} %copy.14.refs_0_, s32[4]{0:T(128)} %bitcast.13, s32[1,128]{1,0:T(1,128)} %refs_2_.1, bf16[64,384]{1,0:T(8,128)(2,1)} %bitcast.12, bf16[1024,512]{1,0:T(8,128)(2,1)} %bitcast.7, bf16[512,2048]{1,0:T(8,128)(2,1)} %refs_5_.1, ...), custom_call_target="tpu_custom_call" | custom-call | tf_op jit(solution)/shard_map/pallas_call | solution.py:572
  69.7 0.0 copy-start
  69.7 0.0 copy-start.1
  69.7 2.3 %copy.15 = bf16[1,1024,512]{2,1,0:T(8,128)(2,1)} copy(bf16[1,1024,512]{2,1,0:T(8,128)(2,1)} %bitcast.8) | data formatting | bytes 2097152
  72.0 0.0 copy-done
  72.0 0.7 copy.16
  72.6 0.0 copy-done.1
  72.6 0.6 copy.17
Async XLA Ops:
  69.7 2.3 %copy-start = (bf16[128,512]{1,0:T(8,128)(2,1)S(1)}, bf16[128,512]{1,0:T(8,128)(2,1)}, u32[]{:S(2)}) copy-start(bf16[128,512]{1,0:T(8,128)(2,1)} %get-tuple-element.7) | copy-start | bytes 393220
  69.7 3.0 %copy-start.1 = (f32[64,384]{1,0:T(8,128)S(1)}, f32[64,384]{1,0:T(8,128)}, u32[]{:S(2)}) copy-start(f32[64,384]{1,0:T(8,128)} %get-tuple-element.8) | copy-start | bytes 294916

commit v3 on v2

--- a/solution.py
+++ b/solution.py
@@ -63,9 +63,9 @@
 
 
 def kernel(
-    len_ref, lists_ref, ids_ref, table_hbm, hist_hbm, win_hbm, wout_hbm, gcand_hbm,
+    len_hbm, lists_hbm, ids_hbm, table_hbm, hist_hbm, win_hbm, wout_hbm, gcand_hbm,
     hist_out, cand_out, tgrad_out, *,
-    hist, win, wout, gcand, tabc, tags, tags_i, pick, back, hotc, e_all, disp, eown, eslot,
+    len_ref, lists_ref, ids_ref, hist, win, wout, gcand, tabv, hold, tags, tags_i, pick, back, hotc, e_all, disp, eown, eslot,
     u2, q2, k2, v2, att, catt, outv, pre_own, pre_slot, uc, qc, gmix, gatt, wts, slope, gq, gkv,
     dsend, drecv, share, share_in, csum, fin, coutv, tgv,
     local_sem, out_sem, s_tab, r_tab, s_tag, r_tag, s_tagi, r_tagi, s_own, r_own, s_slot, r_slot,
@@ -77,23 +77,20 @@
     me_u = lax.axis_index("user")
     rows, d = hist.shape
     cand = gcand.shape[0]
-    chunk, vb = tabc.shape[1:]
-    piece = table_hbm.shape[0]
+    chunk = hold.shape[1]
+    piece, vb = tabv.shape
     per = piece // chunk
     gw = d // 2
     n_slot = eslot.shape[1] // chunk
     own_end = rows + cand
     scale = (d // H) ** (-0.5)
     barrier = pltpu.get_barrier_semaphore()
-    holder = me_u // per
+    def chunk_of(k):
+        return lax.rem(k // per + n_item - me_i, n_item) * per + lax.rem(k, per)
+
+    my_chunk = chunk_of(me_u)
+    holder = my_chunk // per
     at_home = holder == me_i
-
-    copies = [
-        pltpu.make_async_copy(hist_hbm, hist, local_sem.at[0]),
-        pltpu.make_async_copy(win_hbm, win, local_sem.at[1]),
-        pltpu.make_async_copy(gcand_hbm, gcand, local_sem.at[2]),
-        pltpu.make_async_copy(wout_hbm, wout, local_sem.at[3]),
-    ]
 
     def peer_i(k):
         return {"item": lax.rem(me_i + k, n_item)}
@@ -102,7 +99,8 @@
         return {"user": lax.rem(me_u + k, n_user)}
 
     def worker(n):
-        return (lax.rem(me_i + n // per, n_item), me_i * per + lax.rem(n, per))
+        row = lax.rem(me_i + n // per, n_item)
+        return (row, lax.rem(me_i + row, n_item) * per + lax.rem(n, per))
 
     def not_me(place):
         return jnp.logical_or(place[0] != me_i, place[1] != me_u)
@@ -110,31 +108,37 @@
     def signal(place):
         pl.semaphore_signal(barrier, inc=1, device_id=place, device_id_type=MESH)
 
-    @pl.loop(1, n_item)
-    def _(k):
+    for k in range(1, n_item):
         signal(peer_i(k))
-
-    @pl.loop(1, n_user)
-    def _(k):
+    for k in range(1, n_user):
         signal(peer_u(k))
-
-    @pl.loop(0, n_user)
-    def _(n):
-        @pl.when(not_me(worker(n)))
-        def _():
-            signal(worker(n))
-
+    for n in range(n_user):
         @pl.when(not_me((holder, n)))
         def _():
             signal((holder, n))
 
-    for c in copies:
+    small = [
+        pltpu.make_async_copy(len_hbm, len_ref, local_sem.at[0]),
+        pltpu.make_async_copy(lists_hbm, lists_ref, local_sem.at[1]),
+        pltpu.make_async_copy(ids_hbm, ids_ref, local_sem.at[2]),
+        pltpu.make_async_copy(table_hbm, tabv, local_sem.at[3]),
+    ]
+    copies = [
+        pltpu.make_async_copy(hist_hbm, hist, local_sem.at[4]),
+        pltpu.make_async_copy(win_hbm, win, local_sem.at[5]),
+        pltpu.make_async_copy(gcand_hbm, gcand, local_sem.at[6]),
+        pltpu.make_async_copy(wout_hbm, wout, local_sem.at[7]),
+    ]
+    for c in small + copies:
         c.start()
+    for c in small:
+        c.wait()
+    length = len_ref[0]
 
     lane = lax.broadcasted_iota(jnp.int32, (1, cand), 1)
     key_row = jnp.zeros((1, cand), jnp.int32)
     for t in range(n_slot):
-        key_row = jnp.where(lane // chunk == t, lists_ref[t] * chunk + lane - t * chunk, key_row)
+        key_row = jnp.where(lane // chunk == t, lists_ref[0, t] * chunk + lane - t * chunk, key_row)
     tag = jnp.concatenate([ids_ref[...], key_row, jnp.zeros((6, cand), jnp.int32)], 0)
     tags[me_u] = tag
     tags_i[me_i] = tag
@@ -150,24 +154,27 @@
     def tagi_copy(k):
         return remote(tags_i.at[me_i], tags_i.at[me_i], s_tagi.at[k], r_tagi.at[k], peer_i(k))
 
+    def row_of(n):
+        return lax.rem(me_i + n // per, n_item)
+
     def tab_copy(n):
-        at = pl.ds(pl.multiple_of(lax.rem(n, per) * chunk, chunk), chunk)
-        return remote(table_hbm.at[at], tabc.at[me_u], s_tab.at[n], r_tab.at[me_u], worker(n))
+        return remote(hold.at[row_of(n) * per + n % per], e_all.at[me_u], s_tab.at[n],
+                      r_tab.at[me_u], worker(n))
 
     def tab_arrival(u):
-        return remote(tabc.at[u], tabc.at[u], s_tab.at[u], r_tab.at[u], (holder, u))
+        return remote(e_all.at[u], e_all.at[u], s_tab.at[u], r_tab.at[u], (holder, u))
 
     def own_copy(k):
         to = lax.rem(me_u + k, n_user)
-        return remote(e_all.at[to], eown.at[me_u], s_own.at[k], r_own.at[k], peer_u(k))
+        return remote(e_all.at[to], eown.at[my_chunk], s_own.at[k], r_own.at[k], peer_u(k))
 
     def slot_copy(k):
         to = lax.rem(me_u + k, n_user)
-        return remote(disp.at[to], eslot.at[me_u], s_slot.at[k], r_slot.at[k], peer_u(k))
+        return remote(disp.at[to], eslot.at[my_chunk], s_slot.at[k], r_slot.at[k], peer_u(k))
 
     def back_copy(k):
         to = lax.rem(me_u + k, n_user)
-        return remote(dsend.at[to], drecv.at[me_u], s_back.at[k], r_back.at[k], peer_u(k))
+        return remote(dsend.at[chunk_of(to)], drecv.at[me_u], s_back.at[k], r_back.at[k], peer_u(k))
 
     def share_copy(k):
         to = lax.rem(me_i + k, n_item)
@@ -177,39 +184,27 @@
         n = me_i * per + lax.rem(me_u, per)
         return remote(csum.at[r], fin.at[n], s_fin.at[r], r_fin.at[n], (holder, r))
 
+    def fin_from(n):
+        row = n // per
+        return (row, lax.rem(me_i + row, n_item) * per + lax.rem(n, per))
+
     def fin_arrival(n):
-        return remote(fin.at[n], fin.at[n], s_fin.at[n], r_fin.at[n], (n // per, me_i * per + n % per))
-
-    home_at = pl.ds(pl.multiple_of(lax.rem(me_u, per) * chunk, chunk), chunk)
-    home_copy = pltpu.make_async_copy(table_hbm.at[home_at], tabc.at[me_u], local_sem.at[4])
-
-    pl.semaphore_wait(
-        barrier, n_item + 3 * n_user - 2 - 2 * at_home.astype(jnp.int32))
-
-    @pl.loop(0, n_user)
-    def _(n):
-        @pl.when(not_me(worker(n)))
-        def _():
-            tab_copy(n).start()
-
-    @pl.when(at_home)
-    def _():
-        home_copy.start()
+        return remote(fin.at[n], fin.at[n], s_fin.at[n], r_fin.at[n], fin_from(n))
+
+    pl.semaphore_wait(barrier, n_item + 2 * n_user - 2 - at_home.astype(jnp.int32))
+
+    @pl.loop(1, n_item)
+    def _(k):
+        tagi_copy(k).start()
 
     @pl.loop(1, n_user)
     def _(k):
         tag_copy(k).start()
 
-    @pl.loop(1, n_item)
-    def _(k):
-        tagi_copy(k).start()
-
-    length = len_ref[0]
     for c in copies:
         c.wait()
 
-    @pl.loop(0, rows // QB)
-    def _(b):
+    def project(b):
         at = pl.ds(pl.multiple_of(b * QB, QB), QB)
         x = hist[at]
         keep = (b * QB + lax.broadcasted_iota(jnp.int32, (QB, 1), 0)) < length
@@ -221,6 +216,31 @@
             q2[g, at] = silu(nn(x, win[:, 2 * d + c : 2 * d + c + gw])).astype(BF16) * (scale / 2)
             k2[g, at] = silu(nn(x, win[:, 3 * d + c : 3 * d + c + gw])).astype(BF16)
 
+    half = rows // QB // 2
+    pl.loop(0, half)(project)
+
+    @pl.loop(1, n_item)
+    def _(k):
+        tagi_copy(k).wait_recv()
+
+    for i in range(n_item):
+        at = lax.broadcasted_iota(jnp.int32, (vb, cand), 0)
+        hot = jnp.where(at == tags_i[i, 0:1], 1.0, 0.0).astype(BF16)
+        found = nn(tabv[...], hot).astype(BF16)
+        for p in range(per):
+            hold[i * per + p] = found[p * chunk : (p + 1) * chunk]
+
+    for n in range(n_user):
+        @pl.when(not_me(worker(n)))
+        def _():
+            tab_copy(n).start()
+
+    @pl.when(at_home)
+    def _():
+        e_all[me_u] = hold[me_i * per + lax.rem(me_u, per)]
+
+    pl.loop(half, rows // QB)(project)
+
     gmix[...] = nt(gcand[...], wout[...])
 
     @pl.loop(1, n_user)
@@ -231,12 +251,9 @@
     keys_t = jnp.transpose(keys.astype(F32)).astype(jnp.int32)
     line = n_slot * chunk
     col = lax.broadcasted_iota(jnp.int32, (line, n_user * chunk), 1)
-    row = lax.broadcasted_iota(jnp.int32, (n_user * chunk, line), 0)
     for u in range(n_user):
         pick[u * line : (u + 1) * line] = jnp.where(
             col == keys_t[:, u : u + 1], 1.0, 0.0).astype(BF16)
-        back[:, u * line : (u + 1) * line] = jnp.where(
-            row == keys[u : u + 1], 1.0, 0.0).astype(BF16)
 
     @pl.loop(0, n_user)
     def _(u):
@@ -244,17 +261,7 @@
         def _():
             tab_arrival(u).wait_recv()
 
-    @pl.when(at_home)
-    def _():
-        home_copy.wait()
-
-    @pl.loop(0, n_user)
-    def _(u):
-        at = lax.broadcasted_iota(jnp.int32, (vb, cand), 0)
-        hot = jnp.where(at == tags[u, 0:1], 1.0, 0.0).astype(BF16)
-        e_all[u] = nn(tabc[u], hot).astype(BF16)
-
-    eown[me_u] = e_all[me_u]
+    eown[my_chunk] = e_all[me_u]
 
     @pl.loop(1, n_user)
     def _(k):
@@ -262,11 +269,16 @@
 
     picked = nn(pick[...], e_all[...].reshape(n_user * chunk, cand)).astype(BF16)
     disp[...] = picked.reshape(disp.shape)
-    eslot[me_u] = disp[me_u]
+    eslot[my_chunk] = disp[me_u]
 
     @pl.loop(1, n_user)
     def _(k):
         slot_copy(k).start()
+
+    row = lax.broadcasted_iota(jnp.int32, (n_user * chunk, line), 0)
+    for u in range(n_user):
+        back[:, u * line : (u + 1) * line] = jnp.where(
+            row == tags[u, 1:2], 1.0, 0.0).astype(BF16)
 
     def normalize(a0, a1):
         mean = (jnp.sum(a0, 1, keepdims=True) + jnp.sum(a1, 1, keepdims=True)) / d
@@ -406,7 +418,7 @@
             total = total + nt(win[:, 3 * d + c : 3 * d + c + gw], dk)
         dsend[:, t * chunk : (t + 1) * chunk] = total.astype(BF16).reshape(n_user, chunk, cand)
 
-    drecv[me_u] = dsend[me_u]
+    drecv[me_u] = dsend[my_chunk]
 
     @pl.loop(1, n_user)
     def _(k):
@@ -456,13 +468,12 @@
 
     @pl.when(at_home)
     def _():
-        fin[me_u] = csum[me_u]
+        fin[me_i * per + lax.rem(me_u, per)] = csum[me_u]
 
     outs += [history_block(0)]
 
     @pl.loop(1, n_item)
     def _(k):
-        tagi_copy(k).wait_recv()
         share_copy(k).wait_recv()
 
     ids_t = jnp.concatenate([tags_i[i, 0:1] for i in range(n_item)], 0)
@@ -476,7 +487,7 @@
 
     @pl.loop(0, n_user)
     def _(n):
-        @pl.when(not_me((n // per, me_i * per + lax.rem(n, per))))
+        @pl.when(not_me(fin_from(n)))
         def _():
             fin_arrival(n).wait_recv()
 
@@ -513,6 +524,39 @@
         c.wait()
     cout_copy.wait()
     tg_copy.wait()
+
+
+PARTS = 8
+
+
+def hand_over_kernel(a, b, c, a_out, b_out, c_out, a_v, b_v, c_v, sem_in, sem_out):
+    n = a.shape[0] // PARTS
+    steps = []
+    for j in range(PARTS):
+        at = pl.ds(j * n, n)
+        steps.append((a.at[at], a_v.at[at], a_out.at[at]))
+    steps += [(b, b_v, b_out), (c, c_v, c_out)]
+    loads = [pltpu.make_async_copy(x, v, sem_in.at[j]) for j, (x, v, _) in enumerate(steps)]
+    stores = [pltpu.make_async_copy(v, y, sem_out.at[j]) for j, (_, v, y) in enumerate(steps)]
+    for m in loads:
+        m.start()
+    for m, w in zip(loads, stores):
+        m.wait()
+        w.start()
+    for w in stores:
+        w.wait()
+
+
+def hand_over(*arrays):
+    hbm = pl.BlockSpec(memory_space=pl.ANY)
+    return pl.pallas_call(
+        hand_over_kernel,
+        out_shape=tuple(jax.ShapeDtypeStruct(x.shape, x.dtype) for x in arrays),
+        in_specs=[hbm] * 3,
+        out_specs=(hbm,) * 3,
+        scratch_shapes=[pltpu.VMEM(x.shape, x.dtype) for x in arrays]
+        + [pltpu.SemaphoreType.DMA((PARTS + 2,))] * 2,
+    )(*arrays)
 
 
 def local(history, hist_len, cand_ids, cand_lists, item_table, w_in, w_out, grad_cand):
@@ -526,15 +570,15 @@
     chunk = d // n_user
     n_late = (1 + n_slot) * cand
     n_key = rows + n_late
-    vmem = pl.BlockSpec(memory_space=pltpu.VMEM)
-    smem = pl.BlockSpec(memory_space=pltpu.SMEM)
     hbm = pl.BlockSpec(memory_space=pl.ANY)
     V = pltpu.VMEM
     dma = pltpu.SemaphoreType.DMA
     scratch = dict(
+        len_ref=pltpu.SMEM((1,), jnp.int32), lists_ref=pltpu.SMEM((1, n_slot), jnp.int32),
+        ids_ref=V((1, cand), jnp.int32),
         hist=V((rows, d), BF16), win=V((d, 4 * d), BF16), wout=V((d, d), BF16),
         gcand=V((cand, d), BF16),
-        tabc=V((n_user, chunk, vb), BF16),
+        tabv=V((piece, vb), BF16), hold=V((n_user, chunk, cand), BF16),
         tags=V((n_user, 8, cand), jnp.int32), tags_i=V((n_item, 8, cand), jnp.int32),
         pick=V((n_user * n_slot * chunk, n_user * chunk), BF16),
         back=V((n_user * chunk, n_user * n_slot * chunk), BF16),
@@ -554,7 +598,7 @@
         share=V((n_item, piece, cand), BF16), share_in=V((n_item, piece, cand), BF16),
         csum=V((n_user, chunk, cand), BF16), fin=V((n_user, chunk, cand), BF16),
         coutv=V((cand, d), BF16), tgv=V((piece, vb), F32),
-        local_sem=dma((5,)), out_sem=dma((6,)),
+        local_sem=dma((8,)), out_sem=dma((6,)),
         s_tab=dma((n_user,)), r_tab=dma((n_user,)),
         s_tag=dma((n_user,)), r_tag=dma((n_user,)),
         s_tagi=dma((n_item,)), r_tagi=dma((n_item,)),
@@ -576,14 +620,15 @@
             jax.ShapeDtypeStruct((cand, d), BF16),
             jax.ShapeDtypeStruct((piece, vb), F32),
         ),
-        in_specs=[smem, smem, vmem, hbm, hbm, hbm, hbm, hbm],
+        in_specs=[hbm] * 8,
         out_specs=(hbm, hbm, hbm),
         scratch_shapes=list(scratch.values()),
         compiler_params=pltpu.CompilerParams(
             collective_id=0, has_side_effects=True, vmem_limit_bytes=58 * 1024 * 1024),
     )(
-        hist_len, cand_lists[0], cand_ids, item_table.T, history[0], w_in, w_out, grad_cand[0],
+        hist_len, cand_lists, cand_ids, item_table.T, history[0], w_in, w_out, grad_cand[0],
     )
+    hist_out, cand_out, tgrad = hand_over(hist_out, cand_out, tgrad)
     return hist_out[None], cand_out[None], tgrad.T
 
 

time: 73.6 us -> 59 us (0.80)
  Pallas kernels: 68.4 us -> 57.4 us
  local copies, waits for them, and re-layouts: 3.61 us -> 0 us
    pallas_call x1, Pallas kernels: 68.4 us -> 55.2 us  [local(): pl.pallas_call(body, out_shape=(jax.ShapeDtypeStruct((rows, d), BF16), ja...]
    unnamed x7 -> x0, local copies, waits for them, and re-layouts: 3.61 us -> none
    pallas_call x0 -> x1, Pallas kernels: none -> 2.19 us  [hand_over(): pl.pallas_call(hand_over_kernel, out_shape=tuple((jax.ShapeDtypeStruct(x....]
where the time goes in v3:
time: 59 us; the launch traced here: 58.8 us
  Pallas kernels  57.4 us (97%)
  between operations  1.45 us (2%)
    pallas_call x1, Pallas kernels, local(): pl.pallas_call(body, out_shape=(jax.ShapeDtypeStruct((rows, d), BF16), ja...  55.2 us
    pallas_call x1, Pallas kernels, hand_over(): pl.pallas_call(hand_over_kernel, out_shape=tuple((jax.ShapeDtypeStruct(x....  2.19 us

profile of v3, /device:TPU:1, one launch (start us, length us, event | category | flops | bytes accessed | tf_op | source)
XLA Modules:
  0.0 58.8 jit_solution(5035653394551657895)
XLA Ops:
  1.3 55.2 %shard_map.103 = (bf16[1024,512]{1,0:T(8,128)(2,1)}, bf16[128,512]{1,0:T(8,128)(2,1)}, f32[64,384]{1,0:T(8,128)}) custom-call(s32[1]{0:T(128)S(6)} %copy.11.refs_0_, s32[1,4]{1,0:T(1,128)} %refs_1_.1, s32[1,128]{1,0:T(1,128)} %refs_2_.1, bf16[64,384]{1,0:T(8,128)(2,1)} %bitcast.8, bf16[1024,512]{1,0:T(8,128)(2,1)} %bitcast.6, bf16[512,2048]{1,0:T(8,128)(2,1)} %refs_5_.1, ...), custom_call_target="tpu_custom_call" | custom-call | tf_op jit(solution)/shard_map/pallas_call | solution.py:616
  56.5 2.2 %shard_map.104 = (bf16[1024,512]{1,0:T(8,128)(2,1)}, bf16[128,512]{1,0:T(8,128)(2,1)}, f32[64,384]{1,0:T(8,128)}) custom-call(bf16[1024,512]{1,0:T(8,128)(2,1)} %get-tuple-element.9.a, bf16[128,512]{1,0:T(8,128)(2,1)} %get-tuple-element.10.b, f32[64,384]{1,0:T(8,128)} %get-tuple-element.11.c), custom_call_target="tpu_custom_call" | custom-call | tf_op jit(solution)/shard_map/pallas_call | solution.py:552

commit v4 on v3

--- a/solution.py
+++ b/solution.py
@@ -66,9 +66,9 @@
     len_hbm, lists_hbm, ids_hbm, table_hbm, hist_hbm, win_hbm, wout_hbm, gcand_hbm,
     hist_out, cand_out, tgrad_out, *,
     len_ref, lists_ref, ids_ref, hist, win, wout, gcand, tabv, hold, tags, tags_i, pick, back, hotc, e_all, disp, eown, eslot,
-    u2, q2, k2, v2, att, catt, outv, pre_own, pre_slot, uc, qc, gmix, gatt, wts, slope, gq, gkv,
-    dsend, drecv, share, share_in, csum, fin, coutv, tgv,
-    local_sem, out_sem, s_tab, r_tab, s_tag, r_tag, s_tagi, r_tagi, s_own, r_own, s_slot, r_slot,
+    u2, q2, k2, v2, att, catt, pre_own, pre_slot, uc, qc, gmix, gatt, wts, slope, gq, gkv,
+    dsend, drecv, share, share_in, csum, fin, tgv,
+    local_sem, s_tab, r_tab, s_tag, r_tag, s_tagi, r_tagi, s_own, r_own, s_slot, r_slot,
     s_back, r_back, s_share, r_share, s_fin, r_fin,
 ):
     n_item = lax.axis_size("item")
@@ -77,7 +77,7 @@
     me_u = lax.axis_index("user")
     rows, d = hist.shape
     cand = gcand.shape[0]
-    chunk = hold.shape[1]
+    chunk = e_all.shape[1]
     piece, vb = tabv.shape
     per = piece // chunk
     gw = d // 2
@@ -112,10 +112,6 @@
         signal(peer_i(k))
     for k in range(1, n_user):
         signal(peer_u(k))
-    for n in range(n_user):
-        @pl.when(not_me((holder, n)))
-        def _():
-            signal((holder, n))
 
     small = [
         pltpu.make_async_copy(len_hbm, len_ref, local_sem.at[0]),
@@ -131,17 +127,15 @@
     ]
     for c in small + copies:
         c.start()
-    for c in small:
-        c.wait()
-    length = len_ref[0]
-
-    lane = lax.broadcasted_iota(jnp.int32, (1, cand), 1)
-    key_row = jnp.zeros((1, cand), jnp.int32)
-    for t in range(n_slot):
-        key_row = jnp.where(lane // chunk == t, lists_ref[0, t] * chunk + lane - t * chunk, key_row)
-    tag = jnp.concatenate([ids_ref[...], key_row, jnp.zeros((6, cand), jnp.int32)], 0)
-    tags[me_u] = tag
-    tags_i[me_i] = tag
+
+    def build_tags():
+        lane = lax.broadcasted_iota(jnp.int32, (1, cand), 1)
+        key_row = jnp.zeros((1, cand), jnp.int32)
+        for t in range(n_slot):
+            key_row = jnp.where(lane // chunk == t, lists_ref[0, t] * chunk + lane - t * chunk, key_row)
+        tag = jnp.concatenate([ids_ref[...], key_row, jnp.zeros((6, cand), jnp.int32)], 0)
+        tags[me_u] = tag
+        tags_i[me_i] = ids_ref[...]
 
     def remote(src, dst, send, recv, place):
         return pltpu.make_async_remote_copy(
@@ -152,21 +146,22 @@
         return remote(tags.at[me_u], tags.at[me_u], s_tag.at[k], r_tag.at[k], peer_u(k))
 
     def tagi_copy(k):
-        return remote(tags_i.at[me_i], tags_i.at[me_i], s_tagi.at[k], r_tagi.at[k], peer_i(k))
+        return remote(ids_hbm, tags_i.at[me_i], s_tagi.at[k], r_tagi.at[k], peer_i(k))
 
     def row_of(n):
         return lax.rem(me_i + n // per, n_item)
 
     def tab_copy(n):
-        return remote(hold.at[row_of(n) * per + n % per], e_all.at[me_u], s_tab.at[n],
-                      r_tab.at[me_u], worker(n))
+        part = pl.ds((n % per) * chunk, chunk)
+        return remote(hold.at[row_of(n), part], e_all.at[me_u], s_tab.at[n], r_tab.at[me_u],
+                      worker(n))
 
     def tab_arrival(u):
         return remote(e_all.at[u], e_all.at[u], s_tab.at[u], r_tab.at[u], (holder, u))
 
     def own_copy(k):
-        to = lax.rem(me_u + k, n_user)
-        return remote(e_all.at[to], eown.at[my_chunk], s_own.at[k], r_own.at[k], peer_u(k))
+        to = lax.rem(me_i + k, n_item)
+        return remote(hold.at[to], eown.at[me_i], s_own.at[k], r_own.at[k], peer_i(k))
 
     def slot_copy(k):
         to = lax.rem(me_u + k, n_user)
@@ -191,11 +186,16 @@
     def fin_arrival(n):
         return remote(fin.at[n], fin.at[n], s_fin.at[n], r_fin.at[n], fin_from(n))
 
-    pl.semaphore_wait(barrier, n_item + 2 * n_user - 2 - at_home.astype(jnp.int32))
+    pl.semaphore_wait(barrier, n_item + n_user - 2)
 
     @pl.loop(1, n_item)
     def _(k):
         tagi_copy(k).start()
+
+    for c in small:
+        c.wait()
+    length = len_ref[0]
+    build_tags()
 
     @pl.loop(1, n_user)
     def _(k):
@@ -203,82 +203,6 @@
 
     for c in copies:
         c.wait()
-
-    def project(b):
-        at = pl.ds(pl.multiple_of(b * QB, QB), QB)
-        x = hist[at]
-        keep = (b * QB + lax.broadcasted_iota(jnp.int32, (QB, 1), 0)) < length
-        for g in range(2):
-            c = g * gw
-            u2[g, at] = silu(nn(x, win[:, c : c + gw])).astype(BF16)
-            val = silu(nn(x, win[:, d + c : d + c + gw]))
-            v2[g, at] = jnp.where(keep, val, 0.0).astype(BF16)
-            q2[g, at] = silu(nn(x, win[:, 2 * d + c : 2 * d + c + gw])).astype(BF16) * (scale / 2)
-            k2[g, at] = silu(nn(x, win[:, 3 * d + c : 3 * d + c + gw])).astype(BF16)
-
-    half = rows // QB // 2
-    pl.loop(0, half)(project)
-
-    @pl.loop(1, n_item)
-    def _(k):
-        tagi_copy(k).wait_recv()
-
-    for i in range(n_item):
-        at = lax.broadcasted_iota(jnp.int32, (vb, cand), 0)
-        hot = jnp.where(at == tags_i[i, 0:1], 1.0, 0.0).astype(BF16)
-        found = nn(tabv[...], hot).astype(BF16)
-        for p in range(per):
-            hold[i * per + p] = found[p * chunk : (p + 1) * chunk]
-
-    for n in range(n_user):
-        @pl.when(not_me(worker(n)))
-        def _():
-            tab_copy(n).start()
-
-    @pl.when(at_home)
-    def _():
-        e_all[me_u] = hold[me_i * per + lax.rem(me_u, per)]
-
-    pl.loop(half, rows // QB)(project)
-
-    gmix[...] = nt(gcand[...], wout[...])
-
-    @pl.loop(1, n_user)
-    def _(k):
-        tag_copy(k).wait_recv()
-
-    keys = jnp.concatenate([tags[u, 1:2] for u in range(n_user)], 0)
-    keys_t = jnp.transpose(keys.astype(F32)).astype(jnp.int32)
-    line = n_slot * chunk
-    col = lax.broadcasted_iota(jnp.int32, (line, n_user * chunk), 1)
-    for u in range(n_user):
-        pick[u * line : (u + 1) * line] = jnp.where(
-            col == keys_t[:, u : u + 1], 1.0, 0.0).astype(BF16)
-
-    @pl.loop(0, n_user)
-    def _(u):
-        @pl.when(not_me((holder, u)))
-        def _():
-            tab_arrival(u).wait_recv()
-
-    eown[my_chunk] = e_all[me_u]
-
-    @pl.loop(1, n_user)
-    def _(k):
-        own_copy(k).start()
-
-    picked = nn(pick[...], e_all[...].reshape(n_user * chunk, cand)).astype(BF16)
-    disp[...] = picked.reshape(disp.shape)
-    eslot[my_chunk] = disp[me_u]
-
-    @pl.loop(1, n_user)
-    def _(k):
-        slot_copy(k).start()
-
-    row = lax.broadcasted_iota(jnp.int32, (n_user * chunk, line), 0)
-    for u in range(n_user):
-        back[:, u * line : (u + 1) * line] = jnp.where(
-            row == tags[u, 1:2], 1.0, 0.0).astype(BF16)
 
     def normalize(a0, a1):
         mean = (jnp.sum(a0, 1, keepdims=True) + jnp.sum(a1, 1, keepdims=True)) / d
@@ -317,15 +241,79 @@
         m1 = (n1 * u2[1, lo:n].astype(F32)).astype(BF16)
         out = nn(m0, wout[:gw]) + nn(m1, wout[gw:]) + hist[lo:n].astype(F32)
         keep = (lo + lax.broadcasted_iota(jnp.int32, (QB, 1), 0)) < length
-        outv[lo:n] = jnp.where(keep, out, 0.0).astype(BF16)
-        copy = pltpu.make_async_copy(
-            outv.at[pl.ds(lo, QB)], hist_out.at[pl.ds(lo, QB)], out_sem.at[b])
-        copy.start()
-        return copy
-
-    outs = [history_block(1)]
+        hist_out[lo:n] = jnp.where(keep, out, 0.0).astype(BF16)
+
+    def project(b):
+        at = pl.ds(pl.multiple_of(b * QB, QB), QB)
+        x = hist[at]
+        keep = (b * QB + lax.broadcasted_iota(jnp.int32, (QB, 1), 0)) < length
+        for g in range(2):
+            c = g * gw
+            u2[g, at] = silu(nn(x, win[:, c : c + gw])).astype(BF16)
+            val = silu(nn(x, win[:, d + c : d + c + gw]))
+            v2[g, at] = jnp.where(keep, val, 0.0).astype(BF16)
+            q2[g, at] = silu(nn(x, win[:, 2 * d + c : 2 * d + c + gw])).astype(BF16) * (scale / 2)
+            k2[g, at] = silu(nn(x, win[:, 3 * d + c : 3 * d + c + gw])).astype(BF16)
+
+    half = rows // QB // 2
+    pl.loop(0, half)(project)
+
+    at = lax.broadcasted_iota(jnp.int32, (vb, cand), 0)
+    for j in range(n_item):
+        i = lax.rem(me_i + j, n_item)
+        if j:
+            tagi_copy(n_item - j).wait_recv()
+        hot = jnp.where(at == tags_i[i], 1.0, 0.0).astype(BF16)
+        hold[i] = nn(tabv[...], hot).astype(BF16)
+        for n in range(j * per, (j + 1) * per):
+            @pl.when(not_me(worker(n)))
+            def _():
+                tab_copy(n).start()
+        if j:
+            own_copy(j).start()
+
+    @pl.when(at_home)
+    def _():
+        part = pl.ds(pl.multiple_of(lax.rem(me_u, per) * chunk, chunk), chunk)
+        e_all[me_u] = hold[me_i, part]
+
+    eown[me_i] = hold[me_i]
+    pl.loop(half, rows // QB)(project)
 
     @pl.loop(1, n_user)
+    def _(k):
+        tag_copy(k).wait_recv()
+
+    keys = jnp.concatenate([tags[u, 1:2] for u in range(n_user)], 0)
+    keys_t = jnp.transpose(keys.astype(F32)).astype(jnp.int32)
+    line = n_slot * chunk
+    col = lax.broadcasted_iota(jnp.int32, (line, n_user * chunk), 1)
+    for u in range(n_user):
+        pick[u * line : (u + 1) * line] = jnp.where(
+            col == keys_t[:, u : u + 1], 1.0, 0.0).astype(BF16)
+
+    history_block(0)
+
+    @pl.loop(0, n_user)
+    def _(u):
+        @pl.when(not_me((holder, u)))
+        def _():
+            tab_arrival(u).wait_recv()
+
+    picked = nn(pick[...], e_all[...].reshape(n_user * chunk, cand)).astype(BF16)
+    disp[...] = picked.reshape(disp.shape)
+    eslot[my_chunk] = disp[me_u]
+
+    @pl.loop(1, n_user)
+    def _(k):
+        slot_copy(k).start()
+
+    row = lax.broadcasted_iota(jnp.int32, (n_user * chunk, line), 0)
+    for u in range(n_user):
+        back[:, u * line : (u + 1) * line] = jnp.where(
+            row == tags[u, 1:2], 1.0, 0.0).astype(BF16)
+
+    @pl.loop(1, n_item)
     def _(k):
         own_copy(k).wait_recv()
 
@@ -353,7 +341,9 @@
     def _(g):
         catt[g] = scores(g, 0, own_end)
 
-    outs += [history_block(2)]
+    history_block(1)
+    history_block(2)
+    gmix[...] = nt(gcand[...], wout[...])
 
     @pl.loop(1, n_user)
     def _(k):
@@ -424,9 +414,7 @@
     def _(k):
         back_copy(k).start()
 
-    coutv[...] = (nn(m0, wout[:gw]) + nn(m1, wout[gw:]) + own.astype(F32)).astype(BF16)
-    cout_copy = pltpu.make_async_copy(coutv, cand_out, out_sem.at[4])
-    cout_copy.start()
+    cand_out[...] = (nn(m0, wout[:gw]) + nn(m1, wout[gw:]) + own.astype(F32)).astype(BF16)
 
     @pl.loop(0, 2)
     def _(g):
@@ -451,7 +439,7 @@
     def _(k):
         share_copy(k).start()
 
-    outs += [history_block(3)]
+    history_block(3)
 
     @pl.loop(1, n_user)
     def _(k):
@@ -470,20 +458,17 @@
     def _():
         fin[me_i * per + lax.rem(me_u, per)] = csum[me_u]
 
-    outs += [history_block(0)]
-
     @pl.loop(1, n_item)
     def _(k):
         share_copy(k).wait_recv()
 
-    ids_t = jnp.concatenate([tags_i[i, 0:1] for i in range(n_item)], 0)
+    ids_t = jnp.concatenate([tags_i[i] for i in range(n_item)], 0)
     ids_t = jnp.transpose(ids_t.astype(F32)).astype(jnp.int32)
     col = lax.broadcasted_iota(jnp.int32, (cand, vb), 1)
-    tg = jnp.zeros((piece, vb), F32)
     for i in range(n_item):
         hotc[i] = jnp.where(col == ids_t[:, i : i + 1], 1.0, 0.0).astype(BF16)
-        tg = tg + nn(share_in[i], hotc[i])
-    tgv[...] = tg
+    hot_all = hotc[...].reshape(n_item * cand, vb)
+    tgv[...] = nn(jnp.concatenate([share_in[i] for i in range(n_item)], 1), hot_all)
 
     @pl.loop(0, n_user)
     def _(n):
@@ -491,22 +476,18 @@
         def _():
             fin_arrival(n).wait_recv()
 
-    tg = tgv[...]
-    for i in range(n_item):
-        tg = tg + nn(fin[i * per : (i + 1) * per].reshape(piece, cand), hotc[i])
-    tgv[...] = tg
-    tg_copy = pltpu.make_async_copy(tgv, tgrad_out, out_sem.at[5])
-    tg_copy.start()
+    terms = [fin[i * per : (i + 1) * per].reshape(piece, cand) for i in range(n_item)]
+    tgrad_out[...] = tgv[...] + nn(jnp.concatenate(terms, 1), hot_all)
 
     @pl.loop(1, n_item)
     def _(k):
         tagi_copy(k).wait_send()
+        own_copy(k).wait_send()
         share_copy(k).wait_send()
 
     @pl.loop(1, n_user)
     def _(k):
         tag_copy(k).wait_send()
-        own_copy(k).wait_send()
         slot_copy(k).wait_send()
         back_copy(k).wait_send()
 
@@ -520,31 +501,16 @@
         def _():
             fin_copy(n).wait_send()
 
-    for c in outs:
-        c.wait()
-    cout_copy.wait()
-    tg_copy.wait()
-
-
-PARTS = 8
-
-
-def hand_over_kernel(a, b, c, a_out, b_out, c_out, a_v, b_v, c_v, sem_in, sem_out):
-    n = a.shape[0] // PARTS
-    steps = []
-    for j in range(PARTS):
-        at = pl.ds(j * n, n)
-        steps.append((a.at[at], a_v.at[at], a_out.at[at]))
-    steps += [(b, b_v, b_out), (c, c_v, c_out)]
-    loads = [pltpu.make_async_copy(x, v, sem_in.at[j]) for j, (x, v, _) in enumerate(steps)]
-    stores = [pltpu.make_async_copy(v, y, sem_out.at[j]) for j, (_, v, y) in enumerate(steps)]
-    for m in loads:
+
+def hand_over_kernel(a, b, c, a_out, b_out, c_out, sem):
+    moves = [
+        pltpu.make_async_copy(x, y, sem.at[j])
+        for j, (x, y) in enumerate(((a, a_out), (b, b_out), (c, c_out)))
+    ]
+    for m in moves:
         m.start()
-    for m, w in zip(loads, stores):
+    for m in moves:
         m.wait()
-        w.start()
-    for w in stores:
-        w.wait()
 
 
 def hand_over(*arrays):
@@ -554,8 +520,8 @@
         out_shape=tuple(jax.ShapeDtypeStruct(x.shape, x.dtype) for x in arrays),
         in_specs=[hbm] * 3,
         out_specs=(hbm,) * 3,
-        scratch_shapes=[pltpu.VMEM(x.shape, x.dtype) for x in arrays]
-        + [pltpu.SemaphoreType.DMA((PARTS + 2,))] * 2,
+        scratch_shapes=[pltpu.SemaphoreType.DMA((3,))],
+        compiler_params=pltpu.CompilerParams(vmem_limit_bytes=1024 * 1024),
     )(*arrays)
 
 
@@ -578,16 +544,16 @@
         ids_ref=V((1, cand), jnp.int32),
         hist=V((rows, d), BF16), win=V((d, 4 * d), BF16), wout=V((d, d), BF16),
         gcand=V((cand, d), BF16),
-        tabv=V((piece, vb), BF16), hold=V((n_user, chunk, cand), BF16),
-        tags=V((n_user, 8, cand), jnp.int32), tags_i=V((n_item, 8, cand), jnp.int32),
+        tabv=V((piece, vb), BF16), hold=V((n_item, piece, cand), BF16),
+        tags=V((n_user, 8, cand), jnp.int32), tags_i=V((n_item, 1, cand), jnp.int32),
         pick=V((n_user * n_slot * chunk, n_user * chunk), BF16),
         back=V((n_user * chunk, n_user * n_slot * chunk), BF16),
         hotc=V((n_item, cand, vb), BF16),
         e_all=V((n_user, chunk, cand), BF16), disp=V((n_user, n_slot * chunk, cand), BF16),
-        eown=V((n_user, chunk, cand), BF16), eslot=V((n_user, n_slot * chunk, cand), BF16),
+        eown=V((n_item, piece, cand), BF16), eslot=V((n_user, n_slot * chunk, cand), BF16),
         u2=V((2, rows, gw), BF16), q2=V((2, rows, gw), BF16),
         k2=V((2, n_key, gw), BF16), v2=V((2, n_key, gw), BF16),
-        att=V((2, QB, gw), F32), catt=V((2, cand, gw), F32), outv=V((rows, d), BF16),
+        att=V((2, QB, gw), F32), catt=V((2, cand, gw), F32),
         pre_own=V((cand, 4 * d), F32), pre_slot=V((n_slot, cand, 2 * d), F32),
         uc=V((2, cand, gw), BF16), qc=V((2, cand, gw), BF16), gmix=V((cand, d), F32),
         gatt=V((2, cand, gw), BF16),
@@ -597,12 +563,12 @@
         drecv=V((n_user, n_slot * chunk, cand), BF16),
         share=V((n_item, piece, cand), BF16), share_in=V((n_item, piece, cand), BF16),
         csum=V((n_user, chunk, cand), BF16), fin=V((n_user, chunk, cand), BF16),
-        coutv=V((cand, d), BF16), tgv=V((piece, vb), F32),
-        local_sem=dma((8,)), out_sem=dma((6,)),
+        tgv=V((piece, vb), F32),
+        local_sem=dma((8,)),
         s_tab=dma((n_user,)), r_tab=dma((n_user,)),
         s_tag=dma((n_user,)), r_tag=dma((n_user,)),
         s_tagi=dma((n_item,)), r_tagi=dma((n_item,)),
-        s_own=dma((n_user,)), r_own=dma((n_user,)),
+        s_own=dma((n_item,)), r_own=dma((n_item,)),
         s_slot=dma((n_user,)), r_slot=dma((n_user,)),
         s_back=dma((n_user,)), r_back=dma((n_user,)),
         s_share=dma((n_item,)), r_share=dma((n_item,)),
@@ -616,12 +582,10 @@
     hist_out, cand_out, tgrad = pl.pallas_call(
         body,
         out_shape=(
-            jax.ShapeDtypeStruct((rows, d), BF16),
-            jax.ShapeDtypeStruct((cand, d), BF16),
-            jax.ShapeDtypeStruct((piece, vb), F32),
+            V((rows, d), BF16), V((cand, d), BF16), V((piece, vb), F32),
         ),
         in_specs=[hbm] * 8,
-        out_specs=(hbm, hbm, hbm),
+        out_specs=(pl.BlockSpec(memory_space=pltpu.VMEM),) * 3,
         scratch_shapes=list(scratch.values()),
         compiler_params=pltpu.CompilerParams(
             collective_id=0, has_side_effects=True, vmem_limit_bytes=58 * 1024 * 1024),

time: 59 us -> 56.9 us (0.964)
  Pallas kernels: 57.4 us -> 55.3 us
    pallas_call x1, Pallas kernels: 2.19 us -> 1.06 us  [hand_over(): pl.pallas_call(hand_over_kernel, out_shape=tuple((jax.ShapeDtypeStruct(x....]
    pallas_call x1, Pallas kernels: 55.2 us -> 54.2 us  [local(): pl.pallas_call(body, out_shape=(V((rows, d), BF16), V((cand, d), BF16), V...]
where the time goes in v4:
time: 56.9 us; the launch traced here: 56.8 us
  Pallas kernels  55.3 us (97%)
  between operations  1.45 us (3%)
    pallas_call x1, Pallas kernels, local(): pl.pallas_call(body, out_shape=(V((rows, d), BF16), V((cand, d), BF16), V...  54.2 us

profile of v4, /device:TPU:1, one launch (start us, length us, event | category | flops | bytes accessed | tf_op | source)
XLA Modules:
  0.0 56.8 jit_solution(15084582180743165840)
XLA Ops:
  1.3 54.2 %shard_map.103 = (bf16[1024,512]{1,0:T(8,128)(2,1)S(1)}, bf16[128,512]{1,0:T(8,128)(2,1)S(1)}, f32[64,384]{1,0:T(8,128)S(1)}) custom-call(s32[1]{0:T(128)S(6)} %copy.11.refs_0_, s32[1,4]{1,0:T(1,128)} %refs_1_.1, s32[1,128]{1,0:T(1,128)} %refs_2_.1, bf16[64,384]{1,0:T(8,128)(2,1)} %bitcast.8, bf16[1024,512]{1,0:T(8,128)(2,1)} %bitcast.6, ...), custom_call_target="tpu_custom_call" | custom-call | tf_op jit(solution)/shard_map/pallas_call | solution.py:582
  55.5 1.1 %shard_map.104 = (bf16[1024,512]{1,0:T(8,128)(2,1)}, bf16[128,512]{1,0:T(8,128)(2,1)}, f32[64,384]{1,0:T(8,128)}) custom-call(bf16[1024,512]{1,0:T(8,128)(2,1)S(1)} %get-tuple-element.9.a, bf16[128,512]{1,0:T(8,128)(2,1)S(1)} %get-tuple-element.10.b, f32[64,384]{1,0:T(8,128)S(1)} %get-tuple-element.11.c), custom_call_target="tpu_custom_call" | custom-call | tf_op jit(solution)/shard_map/pallas_call | solution.py:518

commit v5 on v4

--- a/solution.py
+++ b/solution.py
@@ -341,7 +341,6 @@
     def _(g):
         catt[g] = scores(g, 0, own_end)
 
-    history_block(1)
     history_block(2)
     gmix[...] = nt(gcand[...], wout[...])
 
@@ -457,6 +456,8 @@
     @pl.when(at_home)
     def _():
         fin[me_i * per + lax.rem(me_u, per)] = csum[me_u]
+
+    history_block(1)
 
     @pl.loop(1, n_item)
     def _(k):

time: 56.9 us -> 55.3 us (0.972)
  Pallas kernels: 55.3 us -> 53.7 us
    pallas_call x1, Pallas kernels: 54.2 us -> 52.6 us  [local(): pl.pallas_call(body, out_shape=(V((rows, d), BF16), V((cand, d), BF16), V...]
where the time goes in v5:
time: 55.3 us; the launch traced here: 55.1 us
  Pallas kernels  53.7 us (97%)
  between operations  1.45 us (3%)
    pallas_call x1, Pallas kernels, local(): pl.pallas_call(body, out_shape=(V((rows, d), BF16), V((cand, d), BF16), V...  52.6 us

profile of v5, /device:TPU:1, one launch (start us, length us, event | category | flops | bytes accessed | tf_op | source)
XLA Modules:
  0.0 55.1 jit_solution(9699651402878626628)
XLA Ops:
  1.3 52.6 %shard_map.103 = (bf16[1024,512]{1,0:T(8,128)(2,1)S(1)}, bf16[128,512]{1,0:T(8,128)(2,1)S(1)}, f32[64,384]{1,0:T(8,128)S(1)}) custom-call(s32[1]{0:T(128)S(6)} %copy.11.refs_0_, s32[1,4]{1,0:T(1,128)} %refs_1_.1, s32[1,128]{1,0:T(1,128)} %refs_2_.1, bf16[64,384]{1,0:T(8,128)(2,1)} %bitcast.8, bf16[1024,512]{1,0:T(8,128)(2,1)} %bitcast.6, ...), custom_call_target="tpu_custom_call" | custom-call | tf_op jit(solution)/shard_map/pallas_call | solution.py:583
  53.9 1.1 %shard_map.104 = (bf16[1024,512]{1,0:T(8,128)(2,1)}, bf16[128,512]{1,0:T(8,128)(2,1)}, f32[64,384]{1,0:T(8,128)}) custom-call(bf16[1024,512]{1,0:T(8,128)(2,1)S(1)} %get-tuple-element.9.a, bf16[128,512]{1,0:T(8,128)(2,1)S(1)} %get-tuple-element.10.b, f32[64,384]{1,0:T(8,128)S(1)} %get-tuple-element.11.c), custom_call_target="tpu_custom_call" | custom-call | tf_op jit(solution)/shard_map/pallas_call | solution.py:519
